TPU v7x, 32 devices: a whole 2x2x4 slice. The times are simulated.
32 devices in a mesh: view: 8 (over y, x, core), tile: 4 (over z).
Axes of the slice: x: 2, y: 2, z: 4, core: 2. Of those that a mesh axis runs over, the one named last changes fastest.
Arguments:
- centers: bfloat16 [96, 2, 128], P('tile'), may hold values from 4 to 28
- log_scales: bfloat16 [96, 2, 128], P('tile'), may hold values from -4 to -1.5
- correlation: bfloat16 [96, 128], P('tile'), may hold values from -0.59765625 to 0.59765625
- opacity_logit: bfloat16 [96, 128], P('tile'), may hold values from -6.5 to -2
- features: bfloat16 [96, 128, 128], P('tile'), may hold values from -16 to 16
- view_offset: float32 [8, 2], P('view'), may hold values from -3 to 3
- block_list: int32 [8, 8, 8], P('view', 'tile'), may hold values from 0 to 95, as said below
- pad_count: int32 [8, 8], P('view', 'tile'), may hold values from 0 to 7, as said below
- block_home: int32 [96], replicated, may hold values from 0 to 95, as said below
- image_grad: bfloat16 [8, 8, 1024, 128], P('view', 'tile'), may hold values from -6 to 6
Outputs:
- image: bfloat16 [8, 8, 1024, 128], P('view', 'tile')
- grad_centers: float32 [96, 2, 128], P('tile')
- grad_log_scales: float32 [96, 2, 128], P('tile')
- grad_correlation: float32 [96, 128], P('tile')
- grad_opacity: float32 [96, 128], P('tile')
- grad_features: float32 [96, 128, 128], P('tile')
Inputs may be any that keep to these rules, and one draw needn't show every extreme that they name: `block_list`: the 2 lists of one view on one index of tile name at most 5 entries whose blocks lie in one shard of 24 rows (through block_home), padded entries included; in every such list set some shard is named exactly 5 times. Padded entries hold valid ids. `pad_count`: the first tile of every view has no padding. `block_home`: A permutation of the block ids.
All inputs are finite; a program needn't handle non-finite values.
Results may differ from a plain program's by a relative error of at most 0.0055.
Values may be sent and summed in bfloat16 or wider, within the bound.
A program may use at most 64 MiB of HBM per device.

v0:
```python
import jax
import jax.numpy as jnp
from jax import lax
from jax.sharding import PartitionSpec as P

TILE_W = 32


def pixel_grid():
    pixel_index = jnp.arange(TILE_W * TILE_W, dtype=jnp.int32)
    across = (pixel_index % TILE_W).astype(jnp.float32) + 0.5
    downward = (pixel_index // TILE_W).astype(jnp.float32) + 0.5
    return (across, downward)


def render_tile(tensors, alive_mask, offset):
    across, downward = pixel_grid()
    feature_width = tensors[4].shape[-1]

    def block_step(running, block_data):
        log_trans, colors = running
        center, log_scale, correl, opacity, feature, alive_flag = block_data
        delta_x = across[:, None] - (center[0] + offset[0])[None, :]
        delta_y = downward[:, None] - (center[1] + offset[1])[None, :]
        coef_a = jnp.exp(log_scale[0])
        coef_c = jnp.exp(log_scale[1])
        coef_b = correl * jnp.sqrt(coef_a * coef_c)
        quadric = (
            coef_a[None, :] * delta_x * delta_x
            + 2.0 * coef_b[None, :] * delta_x * delta_y
            + coef_c[None, :] * delta_y * delta_y
        )
        alphas = jax.nn.sigmoid(opacity)[None, :] * jnp.exp(-0.5 * quadric) * alive_flag
        log_keep = jnp.log1p(-alphas)
        before = jnp.cumsum(log_keep, axis=1) - log_keep
        weight = (alphas * jnp.exp(log_trans[:, None] + before)).astype(jnp.bfloat16)
        colors = colors + jnp.dot(
            weight, feature.astype(jnp.bfloat16), preferred_element_type=jnp.float32
        )
        log_trans = log_trans + jnp.sum(log_keep, axis=1)
        return ((log_trans, colors), None)

    start_state = (
        jnp.zeros((across.shape[0],), jnp.float32),
        jnp.zeros((across.shape[0], feature_width), jnp.float32),
    )
    (log_trans, colors), unused = lax.scan(
        jax.checkpoint(block_step), start_state, tuple(tensors) + (alive_mask,)
    )
    return colors


def shards(
    centers,
    log_scales,
    correlation,
    opacity_logit,
    features,
    view_offset,
    block_list,
    pad_count,
    block_home,
    image_grad,
):
    tile_count = lax.axis_size("tile")
    shard_blocks = centers.shape[0]
    tiles_here = block_list.shape[1]
    list_length = block_list.shape[2]
    slot_count = tiles_here * list_length
    capacity = (slot_count + tile_count - 1) // tile_count + 1
    buffer_size = tile_count * capacity
    block_ids = block_list.reshape(slot_count)
    storage = jnp.take(block_home, block_ids)
    owner_of = storage // shard_blocks
    local_slot = storage % shard_blocks
    owner_hits = (owner_of[:, None] == jnp.arange(tile_count, dtype=jnp.int32)[None, :]).astype(
        jnp.int32
    )
    earlier = jnp.cumsum(owner_hits, axis=0) - owner_hits
    owner_rank = jnp.sum(earlier * owner_hits, axis=1)
    position = owner_of * capacity + owner_rank
    placing = position[:, None] == jnp.arange(buffer_size, dtype=jnp.int32)[None, :]
    requests = jnp.sum(jnp.where(placing, local_slot[:, None] + 1, 0), axis=0) - 1
    asked_slots = lax.all_to_all(requests, "tile", split_axis=0, concat_axis=0, tiled=True)
    everything = (
        lax.all_gather(centers, "tile", axis=0, tiled=True),
        lax.all_gather(log_scales, "tile", axis=0, tiled=True),
        lax.all_gather(correlation, "tile", axis=0, tiled=True),
        lax.all_gather(opacity_logit, "tile", axis=0, tiled=True),
        lax.all_gather(features, "tile", axis=0, tiled=True),
    )
    picked = tuple((jnp.take(array_in, storage, axis=0) for array_in in everything))
    offset = view_offset[0]
    images = []
    slot_grads = []
    for tile_number in range(tiles_here):
        first_row = tile_number * list_length
        inputs = tuple(
            (
                array_in[first_row : first_row + list_length].astype(jnp.float32)
                for array_in in picked
            )
        )
        alive_mask = (
            jnp.arange(list_length, dtype=jnp.int32) < list_length - pad_count[0, tile_number]
        ).astype(jnp.float32)
        colors, pullback = jax.vjp(
            lambda *tensors: render_tile(tensors, alive_mask, offset), *inputs
        )
        images.append(colors.astype(jnp.bfloat16))
        slot_grads.append(
            tuple((grad_in for grad_in in pullback(image_grad[0, tile_number].astype(jnp.float32))))
        )
    image_out = jnp.stack(images)[None]
    joined_grads = tuple(
        (
            jnp.concatenate([grad_set[member] for grad_set in slot_grads], axis=0)
            for member in range(5)
        )
    )
    placing_float = placing.astype(jnp.float32)
    outbound = tuple(
        (
            jnp.tensordot(placing_float, grad_in, axes=(0, 0), precision=lax.Precision.HIGHEST)
            for grad_in in joined_grads
        )
    )
    returned = (
        lax.all_to_all(outbound[0], "tile", split_axis=0, concat_axis=0, tiled=True),
        lax.all_to_all(outbound[1], "tile", split_axis=0, concat_axis=0, tiled=True),
        lax.all_to_all(outbound[2], "tile", split_axis=0, concat_axis=0, tiled=True),
        lax.all_to_all(outbound[3], "tile", split_axis=0, concat_axis=0, tiled=True),
        lax.all_to_all(outbound[4], "tile", split_axis=0, concat_axis=0, tiled=True),
    )
    picking = (asked_slots[:, None] == jnp.arange(shard_blocks, dtype=jnp.int32)[None, :]).astype(
        jnp.float32
    )
    shard_grads = tuple(
        (
            jnp.tensordot(picking, grad_in, axes=(0, 0), precision=lax.Precision.HIGHEST)
            for grad_in in returned
        )
    )
    totals = lax.psum(
        (shard_grads[0], shard_grads[1], shard_grads[2], shard_grads[3], shard_grads[4]), "view"
    )
    return (image_out, totals[0], totals[1], totals[2], totals[3], totals[4])


def solution(mesh):
    in_specs = (
        P("tile", None, None),
        P("tile", None, None),
        P("tile", None),
        P("tile", None),
        P("tile", None, None),
        P("view", None),
        P("view", "tile", None),
        P("view", "tile"),
        P(),
        P("view", "tile", None, None),
    )
    out_specs = (
        P("view", "tile", None, None),
        P("tile", None, None),
        P("tile", None, None),
        P("tile", None),
        P("tile", None),
        P("tile", None, None),
    )
    return jax.shard_map(shards, mesh=mesh, in_specs=in_specs, out_specs=out_specs, check_vma=False)
```

profile of v0, /device:TPU:0, one launch (start us, length us, event | category | flops | bytes accessed | tf_op | source)
XLA Modules:
  0.0 808.1 jit_solution(17665307962321128795)
XLA Ops:
  11.3 6.3 all-to-all-start
  17.6 14.1 %all_gather.18 = bf16[96,128]{1,0:T(8,128)(2,1)S(1)} all-gather(bf16[24,128]{1,0:T(8,128)(2,1)} %param.24), channel_id=1, replica_groups=mesh['view'=8,'tile'=4] {'tile'}, dimensions={0}, use_global_device_ids=true | all-gather | bytes 30720 | tf_op jit(solution)/shard_map/all_gather | solution.py:88
  32.3 13.5 %all_gather.15 = bf16[96,128]{1,0:T(8,128)(2,1)S(1)} all-gather(bf16[24,128]{1,0:T(8,128)(2,1)} %param.25), channel_id=1, replica_groups=mesh['view'=8,'tile'=4] {'tile'}, dimensions={0}, use_global_device_ids=true | all-gather | bytes 30720 | tf_op jit(solution)/shard_map/all_gather | solution.py:89
  46.4 13.7 %all_gather.17 = bf16[96,2,128]{2,1,0:T(2,128)(2,1)S(1)} all-gather(bf16[24,2,128]{2,1,0:T(2,128)(2,1)} %param.22), channel_id=1, replica_groups=mesh['view'=8,'tile'=4] {'tile'}, dimensions={0}, use_global_device_ids=true | all-gather | bytes 61440 | tf_op jit(solution)/shard_map/all_gather | solution.py:86
  60.7 13.6 %all_gather.16 = bf16[96,2,128]{2,1,0:T(2,128)(2,1)S(1)} all-gather(bf16[24,2,128]{2,1,0:T(2,128)(2,1)S(1)} %copy-done.22), channel_id=1, replica_groups=mesh['view'=8,'tile'=4] {'tile'}, dimensions={0}, use_global_device_ids=true | all-gather | bytes 61440 | tf_op jit(solution)/shard_map/all_gather | solution.py:87
  82.2 58.1 %while.85 = (s32[]{:T(128)}, f32[1024]{0:T(1024)S(1)}, f32[1024,128]{1,0:T(8,128)S(1)}, f32[8,1024]{1,0:T(8,128)S(1)}, f32[8,128]{1,0:T(8,128)}, /*index=5*/f32[...) while((s32[]{:T(128)}, f32[1024]{0:T(1024)S(1)}, ...), condition=%wide.region_7.10_spmd.clone, body=%wide.region_4.9_spmd.clone.sunk | while | flops 54808576 | bytes 3253460 | solution.py:47
  141.1 42.4 %while.84 = (s32[]{:T(128)}, f32[1024]{0:T(1024)S(1)}, f32[1024,128]{1,0:T(8,128)S(1)}, f32[8,1024]{1,0:T(8,128)S(1)}, f32[8,128]{1,0:T(8,128)S(1)}, /*index=5*/...) while((s32[]{:T(128)}, f32[1024]{0:T(1024)S(1)}, ...), condition=%wide.region_3.6_spmd.clone, body=%wide.region_0.5_spmd.clone.sunk | while | flops 54808576 | bytes 3253460 | solution.py:47
  186.1 220.0 %while.87 = (s32[]{:T(128)}, f32[1024]{0:T(1024)S(1)}, bf16[1024,128]{1,0:T(8,128)(2,1)}, f32[8,2,128]{2,0,1:T(8,128)}, f32[8,2,128]{2,0,1:T(8,128)}, /*index=5*...) while((s32[]{:T(128)}, f32[1024]{0:T(1024)S(1)}, ...), condition=%wide.region_32.35_spmd.clone, body=%wide.region_22.34_spmd.clone.sunk | while | flops 113807872 | bytes 16300107 | solution.py:47
  194.2 8.8 %reduce_window_sum.100 = f32[1024,128]{0,1:T(8,128)S(1)} reduce-window(f32[1024,128]{0,1:T(8,128)S(1)} %copy.94, f32[]{:T(128)} %constant.342.clone.1..sunk.3), window={size=1x128 pad=0_0x0_127}, to_apply=%region_25.27 | reduce-window | flops 16646144 | bytes 1048580 | tf_op jit(solution)/shard_map/transpose(jvp())/while/body/eval_jaxpr/checkpoint/jit(cumsum)/reduce_window_sum | solution.py:35
  221.6 8.8 %reduce_window_sum.100 = f32[1024,128]{0,1:T(8,128)S(1)} reduce-window(f32[1024,128]{0,1:T(8,128)S(1)} %copy.94, f32[]{:T(128)} %constant.342.clone.1..sunk.3), window={size=1x128 pad=0_0x0_127}, to_apply=%region_25.27 | reduce-window | flops 16646144 | bytes 1048580 | tf_op jit(solution)/shard_map/transpose(jvp())/while/body/eval_jaxpr/checkpoint/jit(cumsum)/reduce_window_sum | solution.py:35
  249.1 8.8 %reduce_window_sum.100 = f32[1024,128]{0,1:T(8,128)S(1)} reduce-window(f32[1024,128]{0,1:T(8,128)S(1)} %copy.94, f32[]{:T(128)} %constant.342.clone.1..sunk.3), window={size=1x128 pad=0_0x0_127}, to_apply=%region_25.27 | reduce-window | flops 16646144 | bytes 1048580 | tf_op jit(solution)/shard_map/transpose(jvp())/while/body/eval_jaxpr/checkpoint/jit(cumsum)/reduce_window_sum | solution.py:35
  276.5 8.8 %reduce_window_sum.100 = f32[1024,128]{0,1:T(8,128)S(1)} reduce-window(f32[1024,128]{0,1:T(8,128)S(1)} %copy.94, f32[]{:T(128)} %constant.342.clone.1..sunk.3), window={size=1x128 pad=0_0x0_127}, to_apply=%region_25.27 | reduce-window | flops 16646144 | bytes 1048580 | tf_op jit(solution)/shard_map/transpose(jvp())/while/body/eval_jaxpr/checkpoint/jit(cumsum)/reduce_window_sum | solution.py:35
  304.0 8.8 %reduce_window_sum.100 = f32[1024,128]{0,1:T(8,128)S(1)} reduce-window(f32[1024,128]{0,1:T(8,128)S(1)} %copy.94, f32[]{:T(128)} %constant.342.clone.1..sunk.3), window={size=1x128 pad=0_0x0_127}, to_apply=%region_25.27 | reduce-window | flops 16646144 | bytes 1048580 | tf_op jit(solution)/shard_map/transpose(jvp())/while/body/eval_jaxpr/checkpoint/jit(cumsum)/reduce_window_sum | solution.py:35
  331.4 8.8 %reduce_window_sum.100 = f32[1024,128]{0,1:T(8,128)S(1)} reduce-window(f32[1024,128]{0,1:T(8,128)S(1)} %copy.94, f32[]{:T(128)} %constant.342.clone.1..sunk.3), window={size=1x128 pad=0_0x0_127}, to_apply=%region_25.27 | reduce-window | flops 16646144 | bytes 1048580 | tf_op jit(solution)/shard_map/transpose(jvp())/while/body/eval_jaxpr/checkpoint/jit(cumsum)/reduce_window_sum | solution.py:35
  358.9 8.8 %reduce_window_sum.100 = f32[1024,128]{0,1:T(8,128)S(1)} reduce-window(f32[1024,128]{0,1:T(8,128)S(1)} %copy.94, f32[]{:T(128)} %constant.342.clone.1..sunk.3), window={size=1x128 pad=0_0x0_127}, to_apply=%region_25.27 | reduce-window | flops 16646144 | bytes 1048580 | tf_op jit(solution)/shard_map/transpose(jvp())/while/body/eval_jaxpr/checkpoint/jit(cumsum)/reduce_window_sum | solution.py:35
  386.3 8.8 %reduce_window_sum.100 = f32[1024,128]{0,1:T(8,128)S(1)} reduce-window(f32[1024,128]{0,1:T(8,128)S(1)} %copy.94, f32[]{:T(128)} %constant.342.clone.1..sunk.3), window={size=1x128 pad=0_0x0_127}, to_apply=%region_25.27 | reduce-window | flops 16646144 | bytes 1048580 | tf_op jit(solution)/shard_map/transpose(jvp())/while/body/eval_jaxpr/checkpoint/jit(cumsum)/reduce_window_sum | solution.py:35
  409.3 224.2 %while.86 = (s32[]{:T(128)}, f32[1024]{0:T(1024)S(1)}, bf16[1024,128]{1,0:T(8,128)(2,1)}, f32[8,2,128]{2,0,1:T(8,128)}, f32[8,2,128]{2,0,1:T(8,128)}, /*index=5*...) while((s32[]{:T(128)}, f32[1024]{0:T(1024)S(1)}, ...), condition=%wide.region_21.24_spmd.clone, body=%wide.region_11.23_spmd.clone.sunk | while | flops 113807872 | bytes 14067563 | solution.py:47
  416.6 8.8 %reduce_window_sum.98 = f32[1024,128]{0,1:T(8,128)S(1)} reduce-window(f32[1024,128]{0,1:T(8,128)S(1)} %copy.90, f32[]{:T(128)} %constant.342.clone.1..sunk.2), window={size=1x128 pad=0_0x0_127}, to_apply=%region_14.16 | reduce-window | flops 16646144 | bytes 1048580 | tf_op jit(solution)/shard_map/transpose(jvp())/while/body/eval_jaxpr/checkpoint/jit(cumsum)/reduce_window_sum | solution.py:35
  444.6 8.8 %reduce_window_sum.98 = f32[1024,128]{0,1:T(8,128)S(1)} reduce-window(f32[1024,128]{0,1:T(8,128)S(1)} %copy.90, f32[]{:T(128)} %constant.342.clone.1..sunk.2), window={size=1x128 pad=0_0x0_127}, to_apply=%region_14.16 | reduce-window | flops 16646144 | bytes 1048580 | tf_op jit(solution)/shard_map/transpose(jvp())/while/body/eval_jaxpr/checkpoint/jit(cumsum)/reduce_window_sum | solution.py:35
  472.6 8.8 %reduce_window_sum.98 = f32[1024,128]{0,1:T(8,128)S(1)} reduce-window(f32[1024,128]{0,1:T(8,128)S(1)} %copy.90, f32[]{:T(128)} %constant.342.clone.1..sunk.2), window={size=1x128 pad=0_0x0_127}, to_apply=%region_14.16 | reduce-window | flops 16646144 | bytes 1048580 | tf_op jit(solution)/shard_map/transpose(jvp())/while/body/eval_jaxpr/checkpoint/jit(cumsum)/reduce_window_sum | solution.py:35
  500.6 8.8 %reduce_window_sum.98 = f32[1024,128]{0,1:T(8,128)S(1)} reduce-window(f32[1024,128]{0,1:T(8,128)S(1)} %copy.90, f32[]{:T(128)} %constant.342.clone.1..sunk.2), window={size=1x128 pad=0_0x0_127}, to_apply=%region_14.16 | reduce-window | flops 16646144 | bytes 1048580 | tf_op jit(solution)/shard_map/transpose(jvp())/while/body/eval_jaxpr/checkpoint/jit(cumsum)/reduce_window_sum | solution.py:35
  528.6 8.8 %reduce_window_sum.98 = f32[1024,128]{0,1:T(8,128)S(1)} reduce-window(f32[1024,128]{0,1:T(8,128)S(1)} %copy.90, f32[]{:T(128)} %constant.342.clone.1..sunk.2), window={size=1x128 pad=0_0x0_127}, to_apply=%region_14.16 | reduce-window | flops 16646144 | bytes 1048580 | tf_op jit(solution)/shard_map/transpose(jvp())/while/body/eval_jaxpr/checkpoint/jit(cumsum)/reduce_window_sum | solution.py:35
  556.6 8.8 %reduce_window_sum.98 = f32[1024,128]{0,1:T(8,128)S(1)} reduce-window(f32[1024,128]{0,1:T(8,128)S(1)} %copy.90, f32[]{:T(128)} %constant.342.clone.1..sunk.2), window={size=1x128 pad=0_0x0_127}, to_apply=%region_14.16 | reduce-window | flops 16646144 | bytes 1048580 | tf_op jit(solution)/shard_map/transpose(jvp())/while/body/eval_jaxpr/checkpoint/jit(cumsum)/reduce_window_sum | solution.py:35
  584.6 8.8 %reduce_window_sum.98 = f32[1024,128]{0,1:T(8,128)S(1)} reduce-window(f32[1024,128]{0,1:T(8,128)S(1)} %copy.90, f32[]{:T(128)} %constant.342.clone.1..sunk.2), window={size=1x128 pad=0_0x0_127}, to_apply=%region_14.16 | reduce-window | flops 16646144 | bytes 1048580 | tf_op jit(solution)/shard_map/transpose(jvp())/while/body/eval_jaxpr/checkpoint/jit(cumsum)/reduce_window_sum | solution.py:35
  612.6 8.8 %reduce_window_sum.98 = f32[1024,128]{0,1:T(8,128)S(1)} reduce-window(f32[1024,128]{0,1:T(8,128)S(1)} %copy.90, f32[]{:T(128)} %constant.342.clone.1..sunk.2), window={size=1x128 pad=0_0x0_127}, to_apply=%region_14.16 | reduce-window | flops 16646144 | bytes 1048580 | tf_op jit(solution)/shard_map/transpose(jvp())/while/body/eval_jaxpr/checkpoint/jit(cumsum)/reduce_window_sum | solution.py:35
  635.0 4.7 all-to-all-start.3
  641.3 4.0 all-to-all-done.3
  650.2 4.0 all-to-all-done.4
  659.1 4.0 all-to-all-done.1
  680.6 18.7 %all-to-all-done.5 = f32[20,128,128]{2,1,0:T(8,128)S(1)} async-done(((f32[20,128,128]{2,1,0:T(8,128)}), f32[20,128,128]{2,1,0:T(8,128)S(1)}, u32[]{:S(2)}, u32[]{:S(2)}) %all-to-all-start.5) | async-done | bytes 1310752 | tf_op jit(solution)/shard_map/all_to_all | solution.py:133
  704.1 28.6 %all-reduce.14.cloned.1.call-done = (f32[24,2,128]{2,0,1:T(8,128)}, f32[24,2,128]{2,0,1:T(8,128)}, f32[24,128]{1,0:T(8,128)}, f32[24,128]{1,0:T(8,128)}) async-done(((f32[24,2,128]{2,0,1:T(8,128)}, f32[24,2,128]{2,0,1:T(8,128)}, f32[24,128]{1,0:T(8,128)}, f32[24,128]{1,0:T(8,128)}), (f32[24,2,128]{2,0,1:T(8,128)}, f32[24,2,128]{2,0,1:T(8,128)}, f32[24,128]{1,0:T(8,128)}, ...) | async-done | bytes 73744 | tf_op jit(solution)/shard_map/psum | solution.py:144
  735.4 61.7 %all-reduce.12.cloned.1.call-done = f32[24,128,128]{2,0,1:T(8,128)} async-done(((f32[24,128,128]{2,0,1:T(8,128)}), f32[24,128,128]{2,0,1:T(8,128)}) %all-reduce.12.cloned.1.call-update) | async-done | bytes 1572880 | tf_op jit(solution)/shard_map/psum | solution.py:144
  (1085 shorter events, 458.9 us)
Async XLA Ops:
  7.2 53.5 %copy-start.22 = (bf16[24,2,128]{2,1,0:T(2,128)(2,1)S(1)}, bf16[24,2,128]{2,1,0:T(2,128)(2,1)}, u32[]{:S(2)}) copy-start(bf16[24,2,128]{2,1,0:T(2,128)(2,1)} %param.23) | copy-start | bytes 36868
  7.2 67.7 %copy-start.25 = (s32[1,2]{1,0:T(1,128)S(1)}, s32[1,2]{1,0:T(1,128)}, u32[]{:S(2)}) copy-start(s32[1,2]{1,0:T(1,128)} %param.29) | copy-start | bytes 28
  7.2 70.1 %copy-start.12 = (f32[1,2]{1,0:T(1,128)S(1)}, f32[1,2]{1,0:T(1,128)}, u32[]{:S(2)}) copy-start(f32[1,2]{1,0:T(1,128)} %param.27) | copy-start | bytes 28
  7.2 71.5 %copy-start.7 = (bf16[1,2,1024,128]{3,2,1,0:T(8,128)(2,1)S(1)}, bf16[1,2,1024,128]{3,2,1,0:T(8,128)(2,1)}, u32[]{:S(2)}) copy-start(bf16[1,2,1024,128]{3,2,1,0:T(8,128)(2,1)} %param.31) | copy-start | bytes 1572868
  7.2 72.3 %all-gather.2.cloned.1.call-start = ((), (), s32[]{:S(2)}) async-start(), calls=%async_computation.6 | async-start | bytes 3932160 | tf_op jit(solution)/shard_map/all_gather | solution.py:90
  11.3 623.8 %all-to-all-start = ((s32[4,5,1]{1,2,0:T(1,128)}), s32[4,5,1]{1,2,0:T(1,128)}, u32[]{:S(2)}, u32[]{:S(2)}) async-start(s32[4,5,1]{1,2,0:T(1,128)} %bitcast.10), calls=%async_computation | async-start | bytes 4096 | tf_op jit(solution)/shard_map/all_to_all | solution.py:84
  205.3 8.3 %copy-start.2 = (bf16[8,128,128]{2,1,0:T(8,128)(2,1)S(1)}, bf16[8,128,128]{2,1,0:T(8,128)(2,1)}, u32[]{:S(2)}) copy-start(bf16[8,128,128]{2,1,0:T(8,128)(2,1)} %copy-done.1) | copy-start | bytes 786436 | tf_op jit(solution)/shard_map/transpose(jvp())/while
  205.4 8.3 %copy-start.14 = (f32[8,2,128]{2,1,0:T(2,128)S(1)}, f32[8,2,128]{2,1,0:T(2,128)}, u32[]{:S(2)}) copy-start(f32[8,2,128]{2,1,0:T(2,128)} %copy-done.13) | copy-start | bytes 24580 | tf_op jit(solution)/shard_map/transpose(jvp())/while
  232.8 8.3 %copy-start.2 = (bf16[8,128,128]{2,1,0:T(8,128)(2,1)S(1)}, bf16[8,128,128]{2,1,0:T(8,128)(2,1)}, u32[]{:S(2)}) copy-start(bf16[8,128,128]{2,1,0:T(8,128)(2,1)} %copy-done.1) | copy-start | bytes 786436 | tf_op jit(solution)/shard_map/transpose(jvp())/while
  232.8 8.3 %copy-start.14 = (f32[8,2,128]{2,1,0:T(2,128)S(1)}, f32[8,2,128]{2,1,0:T(2,128)}, u32[]{:S(2)}) copy-start(f32[8,2,128]{2,1,0:T(2,128)} %copy-done.13) | copy-start | bytes 24580 | tf_op jit(solution)/shard_map/transpose(jvp())/while
  260.2 8.3 %copy-start.2 = (bf16[8,128,128]{2,1,0:T(8,128)(2,1)S(1)}, bf16[8,128,128]{2,1,0:T(8,128)(2,1)}, u32[]{:S(2)}) copy-start(bf16[8,128,128]{2,1,0:T(8,128)(2,1)} %copy-done.1) | copy-start | bytes 786436 | tf_op jit(solution)/shard_map/transpose(jvp())/while
  260.3 8.3 %copy-start.14 = (f32[8,2,128]{2,1,0:T(2,128)S(1)}, f32[8,2,128]{2,1,0:T(2,128)}, u32[]{:S(2)}) copy-start(f32[8,2,128]{2,1,0:T(2,128)} %copy-done.13) | copy-start | bytes 24580 | tf_op jit(solution)/shard_map/transpose(jvp())/while
  287.7 8.3 %copy-start.2 = (bf16[8,128,128]{2,1,0:T(8,128)(2,1)S(1)}, bf16[8,128,128]{2,1,0:T(8,128)(2,1)}, u32[]{:S(2)}) copy-start(bf16[8,128,128]{2,1,0:T(8,128)(2,1)} %copy-done.1) | copy-start | bytes 786436 | tf_op jit(solution)/shard_map/transpose(jvp())/while
  315.1 8.3 %copy-start.2 = (bf16[8,128,128]{2,1,0:T(8,128)(2,1)S(1)}, bf16[8,128,128]{2,1,0:T(8,128)(2,1)}, u32[]{:S(2)}) copy-start(bf16[8,128,128]{2,1,0:T(8,128)(2,1)} %copy-done.1) | copy-start | bytes 786436 | tf_op jit(solution)/shard_map/transpose(jvp())/while
  315.2 8.3 %copy-start.14 = (f32[8,2,128]{2,1,0:T(2,128)S(1)}, f32[8,2,128]{2,1,0:T(2,128)}, u32[]{:S(2)}) copy-start(f32[8,2,128]{2,1,0:T(2,128)} %copy-done.13) | copy-start | bytes 24580 | tf_op jit(solution)/shard_map/transpose(jvp())/while
  315.2 8.3 %copy-start.16 = (f32[8,2,128]{2,1,0:T(2,128)S(1)}, f32[8,2,128]{2,1,0:T(2,128)}, u32[]{:S(2)}) copy-start(f32[8,2,128]{2,1,0:T(2,128)} %copy-done.15) | copy-start | bytes 24580 | tf_op jit(solution)/shard_map/transpose(jvp())/while
  342.6 8.3 %copy-start.2 = (bf16[8,128,128]{2,1,0:T(8,128)(2,1)S(1)}, bf16[8,128,128]{2,1,0:T(8,128)(2,1)}, u32[]{:S(2)}) copy-start(bf16[8,128,128]{2,1,0:T(8,128)(2,1)} %copy-done.1) | copy-start | bytes 786436 | tf_op jit(solution)/shard_map/transpose(jvp())/while
  342.6 8.3 %copy-start.14 = (f32[8,2,128]{2,1,0:T(2,128)S(1)}, f32[8,2,128]{2,1,0:T(2,128)}, u32[]{:S(2)}) copy-start(f32[8,2,128]{2,1,0:T(2,128)} %copy-done.13) | copy-start | bytes 24580 | tf_op jit(solution)/shard_map/transpose(jvp())/while
  370.1 8.3 %copy-start.2 = (bf16[8,128,128]{2,1,0:T(8,128)(2,1)S(1)}, bf16[8,128,128]{2,1,0:T(8,128)(2,1)}, u32[]{:S(2)}) copy-start(bf16[8,128,128]{2,1,0:T(8,128)(2,1)} %copy-done.1) | copy-start | bytes 786436 | tf_op jit(solution)/shard_map/transpose(jvp())/while
  370.1 8.3 %copy-start.14 = (f32[8,2,128]{2,1,0:T(2,128)S(1)}, f32[8,2,128]{2,1,0:T(2,128)}, u32[]{:S(2)}) copy-start(f32[8,2,128]{2,1,0:T(2,128)} %copy-done.13) | copy-start | bytes 24580 | tf_op jit(solution)/shard_map/transpose(jvp())/while
  397.5 8.3 %copy-start.2 = (bf16[8,128,128]{2,1,0:T(8,128)(2,1)S(1)}, bf16[8,128,128]{2,1,0:T(8,128)(2,1)}, u32[]{:S(2)}) copy-start(bf16[8,128,128]{2,1,0:T(8,128)(2,1)} %copy-done.1) | copy-start | bytes 786436 | tf_op jit(solution)/shard_map/transpose(jvp())/while
  397.5 8.3 %copy-start.14 = (f32[8,2,128]{2,1,0:T(2,128)S(1)}, f32[8,2,128]{2,1,0:T(2,128)}, u32[]{:S(2)}) copy-start(f32[8,2,128]{2,1,0:T(2,128)} %copy-done.13) | copy-start | bytes 24580 | tf_op jit(solution)/shard_map/transpose(jvp())/while
  409.3 239.3 %copy-start.24 = (f32[8,2,128]{2,0,1:T(8,128)S(1)}, f32[8,2,128]{2,0,1:T(8,128)}, u32[]{:S(2)}) copy-start(f32[8,2,128]{2,0,1:T(8,128)} %get-tuple-element.901) | copy-start | bytes 24580
  635.0 10.3 %all-to-all-start.3 = ((f32[4,5,128]{2,1,0:T(8,128)}), f32[4,5,128]{2,1,0:T(8,128)S(1)}, u32[]{:S(2)}, u32[]{:S(2)}) async-start(f32[4,5,128]{2,1,0:T(8,128)} %all_to_all.32), calls=%async_computation.3 | async-start | bytes 32768 | tf_op jit(solution)/shard_map/all_to_all | solution.py:131
  645.4 8.8 %all-to-all-start.4 = ((f32[4,5,128]{2,1,0:T(8,128)}), f32[4,5,128]{2,1,0:T(8,128)S(1)}, u32[]{:S(2)}, u32[]{:S(2)}) async-start(f32[4,5,128]{2,1,0:T(8,128)} %all_to_all.35), calls=%async_computation.4 | async-start | bytes 32768 | tf_op jit(solution)/shard_map/all_to_all | solution.py:132
  654.2 8.9 %all-to-all-start.1 = ((f32[20,2,128]{2,1,0:T(2,128)}), f32[20,2,128]{2,1,0:T(2,128)S(1)}, u32[]{:S(2)}, u32[]{:S(2)}) async-start(f32[20,2,128]{2,1,0:T(2,128)} %copy.49), calls=%async_computation.1 | async-start | bytes 40960 | tf_op jit(solution)/shard_map/all_to_all | solution.py:129
  663.1 9.0 %all-to-all-start.2 = ((f32[20,2,128]{2,1,0:T(2,128)}), f32[20,2,128]{2,1,0:T(2,128)S(1)}, u32[]{:S(2)}, u32[]{:S(2)}) async-start(f32[20,2,128]{2,1,0:T(2,128)} %copy.53), calls=%async_computation.2 | async-start | bytes 40960 | tf_op jit(solution)/shard_map/all_to_all | solution.py:130
  672.0 27.3 %all-to-all-start.5 = ((f32[20,128,128]{2,1,0:T(8,128)}), f32[20,128,128]{2,1,0:T(8,128)S(1)}, u32[]{:S(2)}, u32[]{:S(2)}) async-start(f32[20,128,128]{2,1,0:T(8,128)} %copy.57), calls=%async_computation.5 | async-start | bytes 2621440 | tf_op jit(solution)/shard_map/all_to_all | solution.py:133
  675.6 57.1 %all-reduce.14.cloned.1.call-start = ((), (), s32[]{:S(2)}) async-start(), calls=%async_computation.8 | async-start | bytes 147456 | tf_op jit(solution)/shard_map/psum | solution.py:144
  680.6 116.5 %all-reduce.12.cloned.1.call-start = ((), (), s32[]{:S(2)}) async-start(), calls=%async_computation.7 | async-start | bytes 3145728 | tf_op jit(solution)/shard_map/psum | solution.py:144
  735.4 64.6 %copy-start.21 = (f32[24,128]{1,0:T(8,128)S(1)}, f32[24,128]{1,0:T(8,128)}, u32[]{:S(2)}) copy-start(f32[24,128]{1,0:T(8,128)} %get-tuple-element.2091) | copy-start | bytes 36868
  735.4 65.2 %copy-start.20 = (f32[24,128]{1,0:T(8,128)S(1)}, f32[24,128]{1,0:T(8,128)}, u32[]{:S(2)}) copy-start(f32[24,128]{1,0:T(8,128)} %get-tuple-element.2092) | copy-start | bytes 36868
  (89 other events, 376.2 us)
Sparse Core Ops, SparseCore 0:
  9.6 68.0 all-gather.1
  680.7 51.9 all-reduce.13
  736.8 60.2 all-reduce.11
where the time goes:
time: 824 us; the launch traced here: 808 us
  other arithmetic  285 us (35%)
  local copies, waits for them, and re-layouts  219 us (27%)
  waiting for transfers between devices  124 us (15%)
  matrix products  79.5 us (10%)
  blocking collectives  54.9 us (7%)
  starting transfers between devices  24.5 us (3%)
  between operations  15.9 us (2%)
    another operation x48, other arithmetic, block_step(): before = jnp.cumsum(log_keep, axis=1) - log_keep  157 us
    dynamic_update_slice x96, local copies, waits for them, and re-layouts, render_tile(): lax.scan(jax.checkpoint(block_step), start_state, tuple(tensors) + (alive...  120 us
    psum x2, waiting for transfers between devices, shards(): lax.psum((shard_grads[0], shard_grads[1], shard_grads[2], shard_grads[3],...  90.3 us
    dot_general x48, matrix products, block_step(): jnp.dot(weight, feature.astype(jnp.bfloat16), preferred_element_type=jnp....  68 us
    log1p x32, other arithmetic, block_step(): log_keep = jnp.log1p(-alphas)  36.6 us
    dynamic_slice x64, local copies, waits for them, and re-layouts, render_tile(): lax.scan(jax.checkpoint(block_step), start_state, tuple(tensors) + (alive...  33.6 us
    reduce_sum x16, other arithmetic, block_step(): coef_c[None, :] * delta_y * delta_y  33 us
    add x16, other arithmetic, block_step(): delta_x = across[:, None] - (center[0] + offset[0])[None, :]  20.8 us
  transfers between devices with their start and end apart: 9, of which 7 were waited for; matrix products, arithmetic and copies ran while one was open for 71% of the time, Pallas kernels for 0%

commit v1 on v0

v1 whole, which is shorter than its diff:
```python
import functools

import jax
import jax.numpy as jnp
from jax import lax
from jax.experimental import pallas as pl
from jax.experimental.pallas import tpu as pltpu
from jax.sharding import PartitionSpec as P

TILE_W = 32
ROWS = 16
LOG2E = 1.4426950408889634
SMEM = pl.BlockSpec(memory_space=pltpu.SMEM)
VMEM = pl.BlockSpec(memory_space=pltpu.VMEM)
ANY = pl.BlockSpec(memory_space=pl.ANY)
MESH = pl.DeviceIdType.MESH


def f32dot(a, b):
    return jnp.dot(a, b, preferred_element_type=jnp.float32)


def transposed(a):
    return a.astype(jnp.float32).T.astype(a.dtype)


def basis_of(pixel, kind):
    half = TILE_W // 2
    k = pixel % TILE_W - half
    j = pixel // TILE_W - half
    out = jnp.where(kind == 0, 1, 0)
    out = jnp.where(kind == 1, k, out)
    out = jnp.where(kind == 2, j, out)
    out = jnp.where(kind == 3, k * k, out)
    out = jnp.where(kind == 4, k * j, out)
    out = jnp.where(kind == 5, j * j, out)
    return out.astype(jnp.float32).astype(jnp.bfloat16)


def gaussian_terms(block, off_x, off_y):
    half = TILE_W // 2 + 0.0
    x = block[0:1] + (off_x - half - 0.5)
    y = block[1:2] + (off_y - half - 0.5)
    a = jnp.exp(block[2:3])
    c = jnp.exp(block[3:4])
    root = jnp.sqrt(a * c)
    b = block[4:5] * root
    return x, y, a, b, c, root


def render_kernel(
    tiles, length, pixels, chunk,
    rows_ref, slot_ref, pad_ref, off_ref, blocks_ref, cot_ref,
    image_ref, out_ref,
    blk, feat_t, coef, basis, basis_t, lower, upper,
    weight, gweight, ratio, moment, dfeat, grads, zero, in_sem, out_sem,
):
    slots = tiles * length
    gauss = blk.shape[2]
    width = blk.shape[1] - ROWS
    pair = 2
    span = pair * gauss
    pairs = length // pair
    chunks = pixels // chunk

    def fetch(s):
        return pltpu.make_async_copy(blocks_ref.at[rows_ref[s]], blk.at[s], in_sem.at[s])

    for s in range(slots):
        fetch(s).start()

    kinds = lax.broadcasted_iota(jnp.int32, basis.shape, 0)
    basis[...] = basis_of(
        lax.broadcasted_iota(jnp.int32, basis.shape, 1), jnp.where(kinds < 24, kinds % 8, 7)
    )
    basis_t[...] = basis_of(
        lax.broadcasted_iota(jnp.int32, basis_t.shape, 0),
        lax.broadcasted_iota(jnp.int32, basis_t.shape, 1),
    )
    row = lax.broadcasted_iota(jnp.int32, lower.shape, 0)
    col = lax.broadcasted_iota(jnp.int32, lower.shape, 1)
    lower[...] = (col < row).astype(jnp.float32).astype(jnp.bfloat16)
    upper[...] = (col > row).astype(jnp.float32).astype(jnp.bfloat16)
    zero[...] = jnp.zeros_like(zero)
    off_x = off_ref[0, 0]
    off_y = off_ref[0, 1]
    for s in range(slots):
        fetch(s).wait()

    def prepare(s, carry):
        block = blk[s, pl.ds(width, ROWS), :].astype(jnp.float32)
        x, y, a, b, c, root = gaussian_terms(block, off_x, off_y)
        tile = s // length
        dead = s - tile * length >= length - pad_ref[0, tile]
        sig = jax.nn.log_sigmoid(block[5:6])
        first = sig - 0.5 * (a * x * x + 2.0 * b * x * y + c * y * y)
        first = jnp.where(dead, -10000.0, first)
        table = jnp.concatenate(
            [first, a * x + b * y, b * x + c * y, -0.5 * a, -b, -0.5 * c,
             jnp.zeros((2, gauss), jnp.float32)], axis=0
        ) * LOG2E
        high = table.astype(jnp.bfloat16).astype(jnp.float32)
        rest = table - high
        mid = rest.astype(jnp.bfloat16).astype(jnp.float32)
        low = rest - mid
        full = jnp.concatenate([high, mid, low, jnp.zeros((8, gauss), jnp.float32)], axis=0)
        coef[pl.ds(pl.multiple_of(s * gauss, gauss), gauss), :] = full.T.astype(jnp.bfloat16)
        return carry

    lax.fori_loop(0, slots, prepare, 0)
    for s in range(slots):
        tile, entry = s // length, s % length
        feat_t[tile, :, entry * gauss:(entry + 1) * gauss] = transposed(blk[s, 0:width, :])

    moment[...] = jnp.zeros_like(moment)
    dfeat[...] = jnp.zeros_like(dfeat)

    def features_of(tile, p):
        first = tile * length + pair * p
        return jnp.concatenate([blk[first + i, 0:width, :] for i in range(pair)], axis=0)

    def step(n, carry):
        tile = n // chunks
        start = pl.multiple_of((n - tile * chunks) * chunk, chunk)
        cot = cot_ref[0, tile, pl.ds(start, chunk), :]
        cot_t = transposed(cot)
        here = basis[:, pl.ds(start, chunk)]
        here_t = basis_t[pl.ds(start, chunk), :]
        log_trans = jnp.zeros((1, chunk), jnp.float32)
        for p in range(pairs):
            rows = slice(p * span, (p + 1) * span)
            base = pl.multiple_of(tile * (length * gauss) + p * span, span)
            alpha = jnp.exp2(f32dot(coef[pl.ds(base, span), :], here))
            keep = 1.0 - alpha
            log_keep = jnp.log2(keep)
            high = log_keep.astype(jnp.bfloat16)
            low = (log_keep - high.astype(jnp.float32)).astype(jnp.bfloat16)
            before = f32dot(lower[...], high) + f32dot(lower[...], low) + log_trans
            w = alpha * jnp.exp2(before)
            log_trans = before[span - 1:span] + log_keep[span - 1:span]
            weight[rows, :] = w.astype(jnp.bfloat16)
            gweight[rows, :] = f32dot(features_of(tile, p), cot_t) * w
            ratio[rows, :] = alpha / keep
        image = f32dot(feat_t[tile], weight[...])
        image_ref[0, tile, pl.ds(start, chunk), :] = image.T.astype(jnp.bfloat16)
        later = jnp.zeros((1, chunk), jnp.float32)
        for p in reversed(range(pairs)):
            rows = slice(p * span, (p + 1) * span)
            base = pl.multiple_of(tile * (length * gauss) + p * span, span)
            gw = gweight[rows, :]
            after = f32dot(upper[...], gw.astype(jnp.bfloat16)) + later
            later = after[0:1] + gw[0:1]
            slope = (gw - after * ratio[rows, :]).astype(jnp.bfloat16)
            moment[pl.ds(base, span), :] += f32dot(slope, here_t)
            dfeat[pl.ds(base, span), :] += f32dot(weight[rows, :], cot)
        return carry

    lax.fori_loop(0, tiles * chunks, step, 0)

    def finish(s, carry):
        base = pl.multiple_of(s * gauss, gauss)
        grads[s, 0:width, :] = dfeat[pl.ds(base, gauss), :].astype(jnp.bfloat16)
        block = blk[s, pl.ds(width, ROWS), :].astype(jnp.float32)
        x, y, a, b, c, root = gaussian_terms(block, off_x, off_y)
        m = moment[pl.ds(base, gauss), :].T
        m0, m1, m2 = m[0:1], m[1:2], m[2:3]
        sx = m1 - x * m0
        sy = m2 - y * m0
        sxx = m[3:4] - 2.0 * x * m1 + x * x * m0
        sxy = m[4:5] - x * m2 - y * m1 + x * y * m0
        syy = m[5:6] - 2.0 * y * m2 + y * y * m0
        table = jnp.concatenate(
            [a * sx + b * sy, b * sx + c * sy,
             -0.5 * (a * sxx + b * sxy), -0.5 * (c * syy + b * sxy),
             -root * sxy, jax.nn.sigmoid(-block[5:6]) * m0,
             jnp.zeros((ROWS - 6, gauss), jnp.float32)], axis=0
        )
        grads[s, pl.ds(width, ROWS), :] = table.astype(jnp.bfloat16)
        return carry

    lax.fori_loop(0, slots, finish, 0)

    spaces = out_ref.shape[0]

    def put(q, carry):
        s = slot_ref[q]

        @pl.when(s >= 0)
        def _():
            pltpu.make_async_copy(grads.at[jnp.maximum(s, 0)], out_ref.at[q], out_sem).start()

        @pl.when(s < 0)
        def _():
            pltpu.make_async_copy(zero, out_ref.at[q], out_sem).start()

        return carry

    lax.fori_loop(0, spaces, put, 0)

    def drain(q, carry):
        pltpu.make_async_copy(zero, out_ref.at[q], out_sem).wait()
        return carry

    lax.fori_loop(0, spaces, drain, 0)


def render(rows, slot_at, pads, offset, blocks, cotangent):
    tiles, pixels = cotangent.shape[1], cotangent.shape[2]
    width, gauss = cotangent.shape[3], blocks.shape[2]
    slots = rows.shape[0]
    length = slots // tiles
    spaces = slot_at.shape[0]
    chunk = 256
    total = slots * gauss
    depth = blocks.shape[1]
    bf, f4 = jnp.bfloat16, jnp.float32
    return pl.pallas_call(
        functools.partial(render_kernel, tiles, length, pixels, chunk),
        out_shape=(
            jax.ShapeDtypeStruct(cotangent.shape, bf),
            jax.ShapeDtypeStruct((spaces, depth, gauss), bf),
        ),
        in_specs=[SMEM, SMEM, SMEM, SMEM, ANY, VMEM],
        out_specs=(VMEM, ANY),
        scratch_shapes=[
            pltpu.VMEM((slots, depth, gauss), bf),
            pltpu.VMEM((tiles, width, length * gauss), bf),
            pltpu.VMEM((total, 32), bf),
            pltpu.VMEM((32, pixels), bf),
            pltpu.VMEM((pixels, 128), bf),
            pltpu.VMEM((2 * gauss, 2 * gauss), bf),
            pltpu.VMEM((2 * gauss, 2 * gauss), bf),
            pltpu.VMEM((length * gauss, chunk), bf),
            pltpu.VMEM((length * gauss, chunk), f4),
            pltpu.VMEM((length * gauss, chunk), f4),
            pltpu.VMEM((total, 128), f4),
            pltpu.VMEM((total, width), f4),
            pltpu.VMEM((slots, depth, gauss), bf),
            pltpu.VMEM((depth, gauss), bf),
            pltpu.SemaphoreType.DMA((slots,)),
            pltpu.SemaphoreType.DMA,
        ],
        compiler_params=pltpu.CompilerParams(vmem_limit_bytes=40 * 2**20),
        name="render",
    )(rows, slot_at, pads, offset, blocks, cotangent)


def plan_kernel(capacity, shard_blocks, list_ref, home_ref, at_ref, slot_ref, req_ref, want, count):
    tile_count = req_ref.shape[0]
    tiles, length = list_ref.shape[1:]
    for o in range(tile_count):
        count[o] = 0

    def clear(q, carry):
        slot_ref[q] = -1
        want[q] = 0
        return carry

    lax.fori_loop(0, tile_count * capacity, clear, 0)

    def place(s, carry):
        tile = s // length
        row = home_ref[list_ref[0, tile, s - tile * length]]
        owner = row // shard_blocks
        rank = count[owner]
        count[owner] = rank + 1
        q = owner * capacity + rank
        at_ref[s] = q
        slot_ref[q] = s
        want[q] = row - owner * shard_blocks + 1
        return carry

    lax.fori_loop(0, tiles * length, place, 0)
    first = lax.axis_index("tile") * capacity
    lane = lax.broadcasted_iota(jnp.int32, req_ref.shape[1:], 1)
    for o in range(tile_count):
        row = jnp.zeros(req_ref.shape[1:], jnp.int32)
        for c in range(capacity):
            row = jnp.where(lane == first + c, want[o * capacity + c], row)
        req_ref[o] = row


def plan(block_list, block_home, tile_count, capacity, shard_blocks):
    slots = block_list.shape[1] * block_list.shape[2]
    spaces = tile_count * capacity
    i4 = jnp.int32
    return pl.pallas_call(
        functools.partial(plan_kernel, capacity, shard_blocks),
        out_shape=(
            jax.ShapeDtypeStruct((slots,), i4),
            jax.ShapeDtypeStruct((spaces,), i4),
            jax.ShapeDtypeStruct((tile_count, 8, 128), i4),
        ),
        in_specs=[SMEM, SMEM],
        out_specs=(SMEM, SMEM, VMEM),
        scratch_shapes=[pltpu.SMEM((spaces,), i4), pltpu.SMEM((tile_count,), i4)],
        name="plan",
    )(block_list, block_home)


def greet(devices):
    barrier = pltpu.get_barrier_semaphore()
    for device in devices:
        pl.semaphore_signal(barrier, inc=1, device_id=device, device_id_type=MESH)
    pl.semaphore_wait(barrier, len(devices))


def remote(src, dst, send, recv, device):
    return pltpu.make_async_remote_copy(
        src_ref=src, dst_ref=dst, send_sem=send, recv_sem=recv,
        device_id=device, device_id_type=MESH,
    )


def fetch_kernel(
    req_ref, centers_ref, scales_ref, corr_ref, opac_ref, feat_ref,
    got_ref, asked_ref,
    req_in, table, par, staged, req_send, req_recv, send, recv, own_sem, table_sem,
):
    tile_count, capacity = got_ref.shape[:2]
    shard_blocks, width, gauss = feat_ref.shape
    me = lax.axis_index("tile")
    peers = [lax.rem(me + d, tile_count) for d in range(tile_count)]
    sources = [lax.rem(me + tile_count - d, tile_count) for d in range(tile_count)]
    greet([{"tile": p} for p in peers[1:]])

    def ask(d):
        return remote(
            req_ref.at[peers[d]], req_in.at[me], req_send.at[d], req_recv.at[me], {"tile": peers[d]}
        )

    def asked_by(d):
        return remote(
            req_ref.at[sources[d]], req_in.at[sources[d]], req_send.at[d],
            req_recv.at[sources[d]], {"tile": sources[d]},
        )

    for d in range(1, tile_count):
        ask(d).start()
    corr = corr_ref[...].astype(jnp.float32)
    opac = opac_ref[...].astype(jnp.float32)
    par[...] = jnp.zeros_like(par)
    for r in range(shard_blocks):
        par[r, 0:2, :] = centers_ref[r].astype(jnp.float32)
        par[r, 2:4, :] = scales_ref[r].astype(jnp.float32)
        par[r, 4:5, :] = corr[r:r + 1]
        par[r, 5:6, :] = opac[r:r + 1]
    wanted = req_ref[me]
    for d in range(1, tile_count):
        asked_by(d).wait_recv()
        wanted = wanted + req_in[sources[d]]
    asked_ref[...] = wanted
    move = pltpu.make_async_copy(asked_ref, table, table_sem)
    move.start()
    move.wait()

    def give(d):
        return remote(staged.at[d], got_ref.at[me], send.at[d], recv.at[me], {"tile": peers[d]})

    def given(d):
        return remote(
            staged.at[d], got_ref.at[sources[d]], send.at[d], recv.at[sources[d]],
            {"tile": sources[d]},
        )

    keep = pltpu.make_async_copy(staged.at[0], got_ref.at[me], own_sem)
    for d in list(range(1, tile_count)) + [0]:
        for c in range(capacity):
            row = jnp.maximum(table[0, peers[d] * capacity + c] - 1, 0)
            staged[d, c, 0:width, :] = feat_ref[row]
            staged[d, c, width:width + ROWS, :] = par[row].astype(jnp.bfloat16)
        if d:
            give(d).start()
        else:
            keep.start()
    keep.wait()
    for d in range(1, tile_count):
        given(d).wait_recv()
    for d in range(1, tile_count):
        give(d).wait_send()
        ask(d).wait_send()


def fetch(req, capacity, centers, log_scales, correlation, opacity_logit, features):
    tile_count = req.shape[0]
    shard_blocks, width, gauss = features.shape
    depth = width + ROWS
    bf = jnp.bfloat16
    dma = pltpu.SemaphoreType.DMA
    return pl.pallas_call(
        fetch_kernel,
        out_shape=(
            jax.ShapeDtypeStruct((tile_count, capacity, depth, gauss), bf),
            jax.ShapeDtypeStruct(req.shape[1:], jnp.int32),
        ),
        in_specs=[VMEM] * 6,
        out_specs=(ANY, VMEM),
        scratch_shapes=[
            pltpu.VMEM(req.shape, jnp.int32),
            pltpu.SMEM(req.shape[1:], jnp.int32),
            pltpu.VMEM((shard_blocks, ROWS, gauss), jnp.float32),
            pltpu.VMEM((tile_count, capacity, depth, gauss), bf),
            dma((tile_count,)), dma((tile_count,)), dma((tile_count,)), dma((tile_count,)),
            dma, dma,
        ],
        compiler_params=pltpu.CompilerParams(
            collective_id=0, has_side_effects=True, vmem_limit_bytes=32 * 2**20
        ),
        name="fetch",
    )(req, centers, log_scales, correlation, opacity_logit, features)


def reduce_kernel(
    shard_blocks, asked_ref, outbound_ref, out_ref,
    landed, total, pair_out, pair_in, chip_out, chip_in, done,
    send, recv, pair_sem, chip_send, chip_recv, done_send, done_recv, mate_send, mate_recv,
):
    tile_count, capacity, depth, gauss = outbound_ref.shape
    cores, chips, part, _ = done.shape
    half = chips * part
    me = lax.axis_index("tile")
    view = lax.axis_index("view")
    core = lax.rem(view, cores)
    chip = view // cores
    mate = {"view": chip * cores + (1 - core)}
    peers = [lax.rem(me + d, tile_count) for d in range(tile_count)]
    sources = [lax.rem(me + tile_count - d, tile_count) for d in range(tile_count)]
    near = [lax.rem(chip + e, chips) for e in range(chips)]
    behind = [lax.rem(chip + chips - e, chips) for e in range(chips)]

    def on_chip(c):
        return {"view": c * cores + core}

    greet([{"tile": p} for p in peers[1:]] + [mate] + [on_chip(c) for c in near[1:]])

    def give(d):
        return remote(
            outbound_ref.at[peers[d]], landed.at[me], send.at[d], recv.at[me], {"tile": peers[d]}
        )

    def given(d):
        return remote(
            outbound_ref.at[sources[d]], landed.at[sources[d]], send.at[d], recv.at[sources[d]],
            {"tile": sources[d]},
        )

    for d in range(1, tile_count):
        give(d).start()
    rows = shard_blocks * depth
    if 2 * half > rows:
        total[rows:2 * half, :] = jnp.zeros((2 * half - rows, gauss), jnp.float32)
    for d in range(tile_count):
        if d:
            given(d).wait_recv()
        place = landed if d else outbound_ref
        source = sources[d]
        marks = [asked_ref[0, source * capacity + c] for c in range(capacity)]

        def add(r, carry):
            at = pl.ds(pl.multiple_of(r * depth, 16), depth)
            acc = total[at, :] if d else jnp.zeros((depth, gauss), jnp.float32)
            for c in range(capacity):
                mark = jnp.where(marks[c] == r + 1, 1.0, 0.0)
                acc = acc + mark * place[source, c].astype(jnp.float32)
            total[at, :] = acc
            return carry

        lax.fori_loop(0, shard_blocks, add, 0)

    def chunk_of(k, c):
        return pl.ds(pl.multiple_of((k * chips + c) * part, 16), part)

    for c in range(chips):
        pair_out[c] = total[chunk_of(1 - core, c), :].astype(jnp.bfloat16)
    pair = remote(pair_out, pair_in, pair_sem.at[0], pair_sem.at[1], mate)
    pair.start()
    pair.wait_recv()

    def to_chip(e):
        return remote(
            chip_out.at[near[e]], chip_in.at[chip], chip_send.at[e], chip_recv.at[chip],
            on_chip(near[e]),
        )

    def from_chip(e):
        return remote(
            chip_out.at[behind[e]], chip_in.at[behind[e]], chip_send.at[e],
            chip_recv.at[behind[e]], on_chip(behind[e]),
        )

    for e in range(1, chips):
        c = near[e]
        chip_out[c] = (
            total[chunk_of(core, c), :] + pair_in[c].astype(jnp.float32)
        ).astype(jnp.bfloat16)
        to_chip(e).start()
    mine = total[chunk_of(core, chip), :] + pair_in[chip].astype(jnp.float32)
    for e in range(1, chips):
        from_chip(e).wait_recv()
        mine = mine + chip_in[behind[e]].astype(jnp.float32)
    done[core, chip] = mine.astype(jnp.bfloat16)

    def spread(e):
        return remote(
            done.at[core, chip], done.at[core, chip], done_send.at[e], done_recv.at[chip],
            on_chip(near[e]),
        )

    def spread_from(e):
        c = behind[e]
        return remote(
            done.at[core, c], done.at[core, c], done_send.at[e], done_recv.at[c], on_chip(c)
        )

    def pass_on(c):
        return remote(done.at[core, c], done.at[core, c], mate_send.at[c], mate_recv.at[c], mate)

    def passed(c):
        return remote(
            done.at[1 - core, c], done.at[1 - core, c], mate_send.at[c], mate_recv.at[c], mate
        )

    for e in range(1, chips):
        spread(e).start()
    pass_on(chip).start()
    for e in range(1, chips):
        spread_from(e).wait_recv()
        pass_on(behind[e]).start()
    for e in range(chips):
        passed(behind[e]).wait_recv()
    for k in range(cores):
        for c in range(chips):
            out_ref[k, c] = done[k, c]
    for e in range(chips):
        pass_on(behind[e]).wait_send()
    for e in range(1, chips):
        spread(e).wait_send()
        to_chip(e).wait_send()
    pair.wait_send()
    for d in range(1, tile_count):
        give(d).wait_send()


def reduce_grads(asked, outbound, shard_blocks, views):
    tile_count, capacity, depth, gauss = outbound.shape
    cores = 2
    chips = views // cores
    part = -(-shard_blocks * depth // (views * 16)) * 16
    bf, f4 = jnp.bfloat16, jnp.float32
    dma = pltpu.SemaphoreType.DMA
    return pl.pallas_call(
        functools.partial(reduce_kernel, shard_blocks),
        out_shape=jax.ShapeDtypeStruct((cores, chips, part, gauss), bf),
        in_specs=[SMEM, VMEM],
        out_specs=VMEM,
        scratch_shapes=[
            pltpu.VMEM(outbound.shape, bf),
            pltpu.VMEM((views * part, gauss), f4),
            pltpu.VMEM((chips, part, gauss), bf),
            pltpu.VMEM((chips, part, gauss), bf),
            pltpu.VMEM((chips, part, gauss), bf),
            pltpu.VMEM((chips, part, gauss), bf),
            pltpu.VMEM((cores, chips, part, gauss), bf),
            dma((tile_count,)), dma((tile_count,)), dma((2,)),
            dma((chips,)), dma((chips,)), dma((chips,)), dma((chips,)),
            dma((chips,)), dma((chips,)),
        ],
        compiler_params=pltpu.CompilerParams(
            collective_id=1, has_side_effects=True, vmem_limit_bytes=32 * 2**20
        ),
        name="reduce_grads",
    )(asked, outbound)


def unpack_kernel(all_ref, centers_ref, scales_ref, corr_ref, opac_ref, feat_ref):
    shard_blocks, width, _ = feat_ref.shape
    depth = width + ROWS
    for r in range(shard_blocks):
        feat_ref[r] = all_ref[r * depth:r * depth + width, :].astype(jnp.float32)
        par = all_ref[r * depth + width:(r + 1) * depth, :].astype(jnp.float32)
        centers_ref[r] = par[0:2]
        scales_ref[r] = par[2:4]
        corr_ref[r:r + 1, :] = par[4:5]
        opac_ref[r:r + 1, :] = par[5:6]


def unpack(everything, shard_blocks, width, gauss):
    f4 = jnp.float32
    return pl.pallas_call(
        unpack_kernel,
        out_shape=(
            jax.ShapeDtypeStruct((shard_blocks, 2, gauss), f4),
            jax.ShapeDtypeStruct((shard_blocks, 2, gauss), f4),
            jax.ShapeDtypeStruct((shard_blocks, gauss), f4),
            jax.ShapeDtypeStruct((shard_blocks, gauss), f4),
            jax.ShapeDtypeStruct((shard_blocks, width, gauss), f4),
        ),
        in_specs=[VMEM],
        out_specs=(VMEM,) * 5,
        compiler_params=pltpu.CompilerParams(vmem_limit_bytes=32 * 2**20),
        name="unpack",
    )(everything)


def shards(
    centers, log_scales, correlation, opacity_logit, features,
    view_offset, block_list, pad_count, block_home, image_grad,
):
    tile_count = lax.axis_size("tile")
    views = lax.axis_size("view")
    shard_blocks, _, gauss = centers.shape
    width = features.shape[2]
    slot_count = block_list.shape[1] * block_list.shape[2]
    capacity = (slot_count + tile_count - 1) // tile_count + 1
    place, slot_at, req = plan(block_list, block_home, tile_count, capacity, shard_blocks)
    got, asked = fetch(
        req, capacity, centers, log_scales, correlation, opacity_logit, features
    )
    blocks = got.reshape((tile_count * capacity,) + got.shape[2:])
    image, outbound = render(place, slot_at, pad_count, view_offset, blocks, image_grad)
    summed = reduce_grads(asked, outbound.reshape(got.shape), shard_blocks, views)
    return (image,) + tuple(unpack(summed.reshape(-1, gauss), shard_blocks, width, gauss))


def solution(mesh):
    in_specs = (
        P("tile", None, None),
        P("tile", None, None),
        P("tile", None),
        P("tile", None),
        P("tile", None, None),
        P("view", None),
        P("view", "tile", None),
        P("view", "tile"),
        P(),
        P("view", "tile", None, None),
    )
    out_specs = (
        P("view", "tile", None, None),
        P("tile", None, None),
        P("tile", None, None),
        P("tile", None),
        P("tile", None),
        P("tile", None, None),
    )
    return jax.shard_map(shards, mesh=mesh, in_specs=in_specs, out_specs=out_specs, check_vma=False)
```

time: 824 us -> 96.2 us (0.12); the launches traced: 808 us -> 94.8 us
  other arithmetic: 285 us -> 0 us
  local copies, waits for them, and re-layouts: 219 us -> 8.3 us
  waiting for transfers between devices: 124 us -> 0 us
  Pallas kernels: 0 us -> 85.8 us
  matrix products: 79.5 us -> 0 us
  blocking collectives: 54.9 us -> 0 us
  starting transfers between devices: 24.5 us -> 0 us
  between operations: 15.9 us -> 0.69 us
    another operation x67 -> x0, other arithmetic: 157 us -> none  [the longest x48 157 us: block_step(): before = jnp.cumsum(log_keep, axis=1) - log_keep]
    dynamic_update_slice x96 -> x0, local copies, waits for them, and re-layouts: 120 us -> none  [render_tile(): lax.scan(jax.checkpoint(block_step), start_state, tuple(tensors) + (alive...]
    psum x2 -> x0, waiting for transfers between devices: 90.3 us -> none  [shards(): lax.psum((shard_grads[0], shard_grads[1], shard_grads[2], shard_grads[3],...]
    pallas_call x0 -> x5, Pallas kernels: none -> 85.8 us  [the longest x1 36.6 us: reduce_grads(): pl.pallas_call(functools.partial(reduce_kernel, shard_blocks), out_shape=...]
    dot_general x58 -> x0, matrix products: 79.5 us -> none  [the longest x48 68 us: block_step(): jnp.dot(weight, feature.astype(jnp.bfloat16), preferred_element_type=jnp....]
    all_gather x4 -> x0, blocking collectives: 54.9 us -> none  [the longest x1 14.1 us: shards(): lax.all_gather(correlation, 'tile', axis=0, tiled=True)]
    log1p x32 -> x0, other arithmetic: 36.6 us -> none  [block_step(): log_keep = jnp.log1p(-alphas)]
    dynamic_slice x64 -> x0, local copies, waits for them, and re-layouts: 33.6 us -> none  [render_tile(): lax.scan(jax.checkpoint(block_step), start_state, tuple(tensors) + (alive...]
  transfers between devices with their start and end apart: 9 -> 0, of which waited for: 7 -> 0; matrix products, arithmetic and copies ran while one was open for 71% -> 0% of each run, Pallas kernels for 0% -> 0%
where the time goes in v1:
time: 96.2 us; the launch traced here: 94.8 us
  Pallas kernels  85.8 us (89%)
  local copies, waits for them, and re-layouts  8.3 us (9%)
    pallas_call x1, Pallas kernels, reduce_grads(): pl.pallas_call(functools.partial(reduce_kernel, shard_blocks), out_shape=...  36.6 us
    pallas_call x1, Pallas kernels, render(): pl.pallas_call(functools.partial(render_kernel, tiles, length, pixels, ch...  23 us
    pallas_call x1, Pallas kernels, fetch(): pl.pallas_call(fetch_kernel, out_shape=(jax.ShapeDtypeStruct((tile_count,...  22.9 us
    unnamed x22, local copies, waits for them, and re-layouts  8.3 us
    pallas_call x1, Pallas kernels, plan(): pl.pallas_call(functools.partial(plan_kernel, capacity, shard_blocks), ou...  2.02 us

profile of v1, /device:TPU:0, one launch (start us, length us, event | category | flops | bytes accessed | tf_op | source)
XLA Modules:
  0.0 94.8 jit_solution(624702133767350982)
XLA Ops:
  0.6 2.0 %plan.1 = (s32[16]{0:T(128)}, s32[20]{0:T(128)}, s32[4,8,128]{2,1,0:T(8,128)}) custom-call(s32[1,2,8]{2,1,0:T(2,128)} %list_ref.1, s32[96]{0:T(128)} %home_ref.1), custom_call_target="tpu_custom_call" | custom-call | tf_op jit(solution)/shard_map/plan/pallas_call | solution.py:287
  2.7 0.0 copy-start
  2.7 1.1 %copy-done = bf16[24,128,128]{2,1,0:T(8,128)(2,1)S(1)} copy-done((bf16[24,128,128]{2,1,0:T(8,128)(2,1)S(1)}, bf16[24,128,128]{2,1,0:T(8,128)(2,1)}, u32[]{:S(2)}) %copy-start) | copy-done | bytes 786456
  3.8 0.0 copy-start.2
  3.8 0.7 copy-done.2
  4.5 0.0 copy-start.3
  4.5 0.7 copy-done.3
  5.2 0.0 copy-start.4
  5.2 0.7 copy-done.4
  5.9 0.0 copy-start.5
  5.9 0.7 copy-done.5
  6.6 0.0 copy-start.6
  6.6 0.7 copy-done.6
  7.3 22.9 %fetch.1 = (bf16[4,5,144,128]{3,2,1,0:T(8,128)(2,1)S(1)}, s32[8,128]{1,0:T(8,128)S(1)}) custom-call(s32[4,8,128]{2,1,0:T(8,128)S(1)} %copy-done.2, bf16[24,2,128]{2,1,0:T(2,128)(2,1)S(1)} %copy-done.3, bf16[24,2,128]{2,1,0:T(2,128)(2,1)S(1)} %copy-done.4, bf16[24,128]{1,0:T(8,128)(2,1)S(1)} %copy-done.5, bf16[24,128]{1,0:T(8,128)(2,1)S(1)} %copy-done.6, ...), custom_call_target="tpu_custom_call" | custom-call | tf_op jit(solution)/shard_map/fetch/pallas_call | solution.py:390
  30.3 0.0 copy-start.1
  30.3 1.0 %copy-done.1 = bf16[1,2,1024,128]{3,2,1,0:T(8,128)(2,1)S(1)} copy-done((bf16[1,2,1024,128]{3,2,1,0:T(8,128)(2,1)S(1)}, bf16[1,2,1024,128]{3,2,1,0:T(8,128)(2,1)}, u32[]{:S(2)}) %copy-start.1) | copy-done | bytes 524312
  31.3 0.0 copy-start.7
  31.3 0.7 copy-done.7
  32.0 0.0 copy-start.8
  32.0 0.7 copy-done.8
  32.6 0.0 copy-start.9
  32.6 0.7 copy-done.9
  33.3 0.0 copy-start.10
  33.3 0.7 copy-done.10
  33.9 23.0 %render.1 = (bf16[1,2,1024,128]{3,2,1,0:T(8,128)(2,1)}, bf16[20,144,128]{2,1,0:T(8,128)(2,1)S(1)}) custom-call(s32[16]{0:T(128)S(1)} %copy-done.9, s32[20]{0:T(128)S(1)} %copy-done.10, s32[1,2]{1,0:T(1,128)S(1)} %copy-done.7, f32[1,2]{1,0:T(1,128)S(1)} %copy-done.8, bf16[20,144,128]{2,1,0:T(8,128)(2,1)S(1)} %bitcast.4, bf16[1,2,1024,128]{3,2,1,0:T(8,128)(2,1)S(1)} %copy-done.1), custom_call_target="tpu_custom_call" | custom-call | tf_op jit(solution)/shard_map/render/pallas_call | solution.py:217
  56.9 36.6 %reduce_grads.1 = bf16[2,4,432,128]{3,2,1,0:T(8,128)(2,1)S(1)} custom-call(s32[8,128]{1,0:T(8,128)S(1)} %get-tuple-element.23.asked_ref, bf16[4,5,144,128]{3,2,1,0:T(8,128)(2,1)S(1)} %bitcast.5), custom_call_target="tpu_custom_call" | custom-call | tf_op jit(solution)/shard_map/reduce_grads/pallas_call | solution.py:551
  93.5 1.3 %unpack.1 = (f32[24,2,128]{2,1,0:T(2,128)}, f32[24,2,128]{2,1,0:T(2,128)}, f32[24,128]{1,0:T(8,128)}, f32[24,128]{1,0:T(8,128)}, f32[24,128,128]{2,1,0:T(8,128)}) custom-call(bf16[3456,128]{1,0:T(8,128)(2,1)S(1)} %bitcast.3), custom_call_target="tpu_custom_call" | custom-call | tf_op jit(solution)/shard_map/unpack/pallas_call | solution.py:589
Async XLA Ops:
  2.7 1.1 %copy-start = (bf16[24,128,128]{2,1,0:T(8,128)(2,1)S(1)}, bf16[24,128,128]{2,1,0:T(8,128)(2,1)}, u32[]{:S(2)}) copy-start(bf16[24,128,128]{2,1,0:T(8,128)(2,1)} %feat_ref.1) | copy-start | bytes 2359300
  3.8 0.7 copy-start.2
  4.5 0.7 copy-start.3
  5.2 0.7 copy-start.4
  5.9 0.7 copy-start.5
  6.6 0.7 copy-start.6
  30.3 1.0 %copy-start.1 = (bf16[1,2,1024,128]{3,2,1,0:T(8,128)(2,1)S(1)}, bf16[1,2,1024,128]{3,2,1,0:T(8,128)(2,1)}, u32[]{:S(2)}) copy-start(bf16[1,2,1024,128]{3,2,1,0:T(8,128)(2,1)} %cot_ref.1) | copy-start | bytes 1572868
  31.3 0.7 copy-start.7
  32.0 0.7 copy-start.8
  32.6 0.7 copy-start.9
  33.3 0.7 copy-start.10

commit v2 on v0

v2 whole, which is shorter than its diff:
```python
import functools

import jax
import jax.numpy as jnp
from jax import lax
from jax.experimental import pallas as pl
from jax.experimental.pallas import tpu as pltpu
from jax.sharding import PartitionSpec as P

TILE_W = 32
ROWS = 16
PAIR = 2
CORES = 2
LOG2E = 1.4426950408889634
SMEM = pl.BlockSpec(memory_space=pltpu.SMEM)
VMEM = pl.BlockSpec(memory_space=pltpu.VMEM)
ANY = pl.BlockSpec(memory_space=pl.ANY)
MESH = pl.DeviceIdType.MESH


def f32dot(a, b):
    return jnp.dot(a, b, preferred_element_type=jnp.float32)


def transposed(a):
    return a.astype(jnp.float32).T.astype(a.dtype)


def basis_of(pixel, kind):
    half = TILE_W // 2
    k = pixel % TILE_W - half
    j = pixel // TILE_W - half
    out = jnp.where(kind == 0, 1, 0)
    out = jnp.where(kind == 1, k, out)
    out = jnp.where(kind == 2, j, out)
    out = jnp.where(kind == 3, k * k, out)
    out = jnp.where(kind == 4, k * j, out)
    out = jnp.where(kind == 5, j * j, out)
    return out.astype(jnp.float32).astype(jnp.bfloat16)


def gaussian_terms(block, off_x, off_y):
    half = TILE_W // 2 + 0.0
    x = block[0:1] + (off_x - half - 0.5)
    y = block[1:2] + (off_y - half - 0.5)
    a = jnp.exp(block[2:3])
    c = jnp.exp(block[3:4])
    root = jnp.sqrt(a * c)
    b = block[4:5] * root
    return x, y, a, b, c, root


def remote(src, dst, send, recv, device):
    return pltpu.make_async_remote_copy(
        src_ref=src, dst_ref=dst, send_sem=send, recv_sem=recv,
        device_id=device, device_id_type=MESH,
    )


def local(src, dst, sem):
    return pltpu.make_async_copy(src, dst, sem)


def splat_kernel(
    capacity, chunk,
    list_hbm, home_hbm, pad_hbm, off_hbm, centers_hbm, scales_hbm, corr_hbm, opac_hbm,
    feat_hbm, cot_hbm,
    image_ref, out_ref,
    list_ref, home_ref, pad_ref, off_ref, centers_ref, scales_ref, corr_ref, opac_ref,
    feat_ref, cot_ref, in_sem,
    at_ref, owner_ref, slot_ref, req, req_in, table_v, table, table_sem, req_send, req_recv,
    par, par_out, par_in, feat_out, feat_in,
    par_send, par_recv, feat_send, feat_recv,
    blk, prm, feat_t, coef, basis, basis_t, lower, upper,
    weight, exact, ratio, moment, dfeat, dpar,
    grad_out, grad_in, dpar_out, dpar_in, grad_send, grad_recv, dpar_send, dpar_recv,
    total, pair_out, pair_in, chip_out, chip_in, done,
    pair_sem, chip_send, chip_recv, done_send, done_recv, mate_send, mate_recv,
):
    _, tiles, length = list_ref.shape
    pixels = cot_ref.shape[2]
    slots = tiles * length
    shard_blocks, gauss, width = feat_ref.shape
    tile_count = req.shape[0]
    depth = gauss + ROWS
    span = PAIR * gauss
    pairs = length // PAIR
    chunks = pixels // chunk
    _, chips, part, _ = done.shape
    half = chips * part
    bf, f4 = jnp.bfloat16, jnp.float32

    me = lax.axis_index("tile")
    view = lax.axis_index("view")
    core = lax.rem(view, CORES)
    chip = view // CORES
    mate = {"view": chip * CORES + (1 - core)}
    peers = [lax.rem(me + d, tile_count) for d in range(tile_count)]
    sources = [lax.rem(me + tile_count - d, tile_count) for d in range(tile_count)]
    near = [lax.rem(chip + e, chips) for e in range(chips)]
    behind = [lax.rem(chip + chips - e, chips) for e in range(chips)]

    def on_chip(c):
        return {"view": c * CORES + core}

    def give(out, into, send, recv, d):
        return remote(out.at[peers[d]], into.at[me], send.at[d], recv.at[me], {"tile": peers[d]})

    def given(out, into, send, recv, d):
        s = sources[d]
        return remote(out.at[s], into.at[s], send.at[d], recv.at[s], {"tile": s})

    ask = (req, req_in, req_send, req_recv)
    pars = (par_out, par_in, par_send, par_recv)
    feats = (feat_out, feat_in, feat_send, feat_recv)
    grads = (grad_out, grad_in, grad_send, grad_recv)
    dpars = (dpar_out, dpar_in, dpar_send, dpar_recv)

    loads = [
        local(src, dst, in_sem.at[n]) for n, (src, dst) in enumerate((
            (list_hbm, list_ref), (home_hbm, home_ref), (pad_hbm, pad_ref), (off_hbm, off_ref),
            (centers_hbm, centers_ref), (scales_hbm, scales_ref), (corr_hbm, corr_ref),
            (opac_hbm, opac_ref), (feat_hbm, feat_ref), (cot_hbm, cot_ref),
        ))
    ]
    for load in loads:
        load.start()
    barrier = pltpu.get_barrier_semaphore()
    others = [{"tile": p} for p in peers[1:]] + [mate] + [on_chip(c) for c in near[1:]]
    for device in others:
        pl.semaphore_signal(barrier, inc=1, device_id=device, device_id_type=MESH)

    loads[0].wait()
    loads[1].wait()
    first = me * capacity
    lane = lax.broadcasted_iota(jnp.int32, req.shape[1:], 1)
    asks = [jnp.zeros(req.shape[1:], jnp.int32) for _ in range(tile_count)]
    owners, places = [], []
    for s in range(slots):
        row = home_ref[list_ref[0, s // length, s % length]]
        owner = row // shard_blocks
        rank = jnp.int32(0)
        for other in owners:
            rank = rank + jnp.where(other == owner, 1, 0)
        owners.append(owner)
        places.append(owner * capacity + rank)
        at_ref[s] = places[s]
        for o in range(tile_count):
            here = jnp.where(owner == o, row - owner * shard_blocks + 1, 0)
            asks[o] = asks[o] + jnp.where(lane == first + rank, here, 0)
    for o in range(tile_count):
        req[o] = asks[o]
    pl.semaphore_wait(barrier, len(others))
    for d in range(1, tile_count):
        give(*ask, d).start()

    for load in loads[2:]:
        load.wait()
    corr = corr_ref[...].astype(f4)
    opac = opac_ref[...].astype(f4)
    par[...] = jnp.zeros_like(par)
    for r in range(shard_blocks):
        par[r, 0:2, :] = centers_ref[r].astype(f4)
        par[r, 2:4, :] = scales_ref[r].astype(f4)
        par[r, 4:5, :] = corr[r:r + 1]
        par[r, 5:6, :] = opac[r:r + 1]
    wanted = req[me]
    for d in range(1, tile_count):
        given(*ask, d).wait_recv()
        wanted = wanted + req_in[sources[d]]
    table_v[...] = wanted
    move = local(table_v, table, table_sem)
    move.start()
    move.wait()

    def wanted_row(d, c):
        return jnp.maximum(table[0, peers[d] * capacity + c] - 1, 0)

    for d in range(1, tile_count):
        for c in range(capacity):
            par_out[peers[d], c] = par[wanted_row(d, c)].astype(bf)
        give(*pars, d).start()
    for d in range(1, tile_count):
        for c in range(capacity):
            feat_out[peers[d], c] = feat_ref[wanted_row(d, c)]
        give(*feats, d).start()
    for c in range(capacity):
        par_in[me, c] = par[wanted_row(0, c)].astype(bf)
        feat_in[me, c] = feat_ref[wanted_row(0, c)]

    kinds = lax.broadcasted_iota(jnp.int32, basis.shape, 0)
    basis[...] = basis_of(
        lax.broadcasted_iota(jnp.int32, basis.shape, 1), jnp.where(kinds < 24, kinds % 8, 7)
    )
    basis_t[...] = basis_of(
        lax.broadcasted_iota(jnp.int32, basis_t.shape, 0),
        lax.broadcasted_iota(jnp.int32, basis_t.shape, 1),
    )
    across = lax.broadcasted_iota(jnp.int32, lower.shape, 0)
    along = lax.broadcasted_iota(jnp.int32, lower.shape, 1)
    lower[...] = (along < across).astype(f4).astype(bf)
    upper[...] = (along > across).astype(f4).astype(bf)
    moment[...] = jnp.zeros_like(moment)
    dfeat[...] = jnp.zeros_like(dfeat)
    for q in range(tile_count * capacity):
        slot = jnp.int32(0)
        for s in range(slots):
            slot = slot + jnp.where(places[s] == q, s + 1, 0)
        slot_ref[q] = slot
    off_x = off_ref[0, 0]
    off_y = off_ref[0, 1]

    def entry(ref, s):
        q = at_ref[s]
        owner = q // capacity
        return ref[owner, q - owner * capacity]

    for d in range(1, tile_count):
        given(*pars, d).wait_recv()

    def prepare(s, carry):
        block = entry(par_in, s).astype(f4)
        prm[s] = block
        x, y, a, b, c, root = gaussian_terms(block, off_x, off_y)
        tile = s // length
        dead = s - tile * length >= length - pad_ref[0, tile]
        sig = jax.nn.log_sigmoid(block[5:6])
        const = sig - 0.5 * (a * x * x + 2.0 * b * x * y + c * y * y)
        const = jnp.where(dead, -10000.0, const)
        terms = jnp.concatenate(
            [const, a * x + b * y, b * x + c * y, -0.5 * a, -b, -0.5 * c,
             jnp.zeros((2, gauss), f4)], axis=0
        ) * LOG2E
        high = terms.astype(bf).astype(f4)
        rest = terms - high
        mid = rest.astype(bf).astype(f4)
        full = jnp.concatenate([high, mid, rest - mid, jnp.zeros((8, gauss), f4)], axis=0)
        coef[pl.ds(pl.multiple_of(s * gauss, gauss), gauss), :] = full.T.astype(bf)
        return carry

    lax.fori_loop(0, slots, prepare, 0)

    def forward(n, carry):
        tile = n // chunks
        start = pl.multiple_of((n - tile * chunks) * chunk, chunk)
        cot = cot_ref[0, tile, pl.ds(start, chunk), :]
        here = basis[:, pl.ds(start, chunk)]
        log_trans = jnp.zeros((1, chunk), f4)
        for p in range(pairs):
            base = pl.multiple_of(tile * (length * gauss) + p * span, span)
            at = (n, pl.ds(p * span, span))
            alpha = jnp.exp2(f32dot(coef[pl.ds(base, span), :], here))
            keep = 1.0 - alpha
            log_keep = jnp.log2(keep)
            high = log_keep.astype(bf)
            low = (log_keep - high.astype(f4)).astype(bf)
            before = f32dot(lower[...], high) + f32dot(lower[...], low) + log_trans
            w = alpha * jnp.exp2(before)
            log_trans = before[span - 1:span] + log_keep[span - 1:span]
            wb = w.astype(bf)
            weight[at] = wb
            exact[at] = w
            ratio[at] = alpha / keep
            slot = tile * length + p * PAIR
            more = f32dot(wb, cot)
            for i in range(PAIR):
                dfeat[slot + i] += more[i * gauss:(i + 1) * gauss]
        return carry

    lax.fori_loop(0, tiles * chunks, forward, 0)

    def outgoing(grad_ref, q):
        slot = slot_ref[q]
        return jnp.where(slot > 0, grad_ref[jnp.maximum(slot - 1, 0)], 0.0)

    for d in list(range(1, tile_count)) + [0]:
        for c in range(capacity):
            got = outgoing(dfeat, peers[d] * capacity + c).astype(bf)
            if d:
                grad_out[peers[d], c] = got
            else:
                grad_in[me, c] = got
        if d:
            give(*grads, d).start()

    for d in range(1, tile_count):
        given(*feats, d).wait_recv()
    for s in range(slots):
        tile, place = s // length, s % length
        feature = entry(feat_in, s)
        blk[s] = feature
        feat_t[tile, :, place * gauss:(place + 1) * gauss] = transposed(feature)

    def backward(n, carry):
        tile = n // chunks
        start = pl.multiple_of((n - tile * chunks) * chunk, chunk)
        cot_t = transposed(cot_ref[0, tile, pl.ds(start, chunk), :])
        here_t = basis_t[pl.ds(start, chunk), :]
        later = jnp.zeros((1, chunk), f4)
        for p in reversed(range(pairs)):
            base = pl.multiple_of(tile * (length * gauss) + p * span, span)
            at = (n, pl.ds(p * span, span))
            slot = tile * length + p * PAIR
            feature = jnp.concatenate([blk[slot + i] for i in range(PAIR)], axis=0)
            gw = f32dot(feature, cot_t) * exact[at]
            after = f32dot(upper[...], gw.astype(bf)) + later
            later = after[0:1] + gw[0:1]
            slope = (gw - after * ratio[at]).astype(bf)
            moment[pl.ds(base, span), :] += f32dot(slope, here_t)
        image = f32dot(feat_t[tile], weight[n])
        image_ref[0, tile, pl.ds(start, chunk), :] = image.T.astype(bf)
        return carry

    lax.fori_loop(0, tiles * chunks, backward, 0)

    def finish(s, carry):
        x, y, a, b, c, root = gaussian_terms(prm[s], off_x, off_y)
        m = moment[pl.ds(pl.multiple_of(s * gauss, gauss), gauss), :].T
        m0, m1, m2 = m[0:1], m[1:2], m[2:3]
        sx = m1 - x * m0
        sy = m2 - y * m0
        sxx = m[3:4] - 2.0 * x * m1 + x * x * m0
        sxy = m[4:5] - x * m2 - y * m1 + x * y * m0
        syy = m[5:6] - 2.0 * y * m2 + y * y * m0
        dpar[s] = jnp.concatenate(
            [a * sx + b * sy, b * sx + c * sy,
             -0.5 * (a * sxx + b * sxy), -0.5 * (c * syy + b * sxy),
             -root * sxy, jax.nn.sigmoid(-prm[s, 5:6, :]) * m0,
             jnp.zeros((2, gauss), f4)], axis=0
        )
        return carry

    lax.fori_loop(0, slots, finish, 0)
    for d in list(range(1, tile_count)) + [0]:
        for c in range(capacity):
            got = outgoing(dpar, peers[d] * capacity + c)
            if d:
                dpar_out[peers[d], c] = got
            else:
                dpar_in[me, c] = got
        if d:
            give(*dpars, d).start()

    total[...] = jnp.zeros_like(total)
    for d in range(tile_count):
        if d:
            given(*grads, d).wait_recv()
        source = sources[d]
        marks = [table[0, source * capacity + c] for c in range(capacity)]

        def add(r, carry):
            at = pl.ds(pl.multiple_of(r * depth, 16), gauss)
            acc = total[at, :]
            for c in range(capacity):
                mark = jnp.where(marks[c] == r + 1, 1.0, 0.0)
                acc = acc + mark * grad_in[source, c].astype(f4)
            total[at, :] = acc
            return carry

        lax.fori_loop(0, shard_blocks, add, 0)
    for d in range(1, tile_count):
        given(*dpars, d).wait_recv()

    def add_par(r, carry):
        acc = jnp.zeros(dpar_in.shape[2:], f4)
        for t in range(tile_count):
            for c in range(capacity):
                mark = jnp.where(table[0, t * capacity + c] == r + 1, 1.0, 0.0)
                acc = acc + mark * dpar_in[t, c]
        total[pl.ds(pl.multiple_of(r * depth + gauss, 16), 8), :] = acc
        return carry

    lax.fori_loop(0, shard_blocks, add_par, 0)

    def chunk_of(k, c):
        return pl.ds(pl.multiple_of((k * chips + c) * part, 16), part)

    for c in range(chips):
        pair_out[c] = total[chunk_of(1 - core, c), :].astype(bf)
    pair = remote(pair_out, pair_in, pair_sem.at[0], pair_sem.at[1], mate)
    pair.start()
    pair.wait_recv()

    def to_chip(e):
        return remote(
            chip_out.at[near[e]], chip_in.at[chip], chip_send.at[e], chip_recv.at[chip],
            on_chip(near[e]),
        )

    def from_chip(e):
        return remote(
            chip_out.at[behind[e]], chip_in.at[behind[e]], chip_send.at[e],
            chip_recv.at[behind[e]], on_chip(behind[e]),
        )

    for e in range(1, chips):
        c = near[e]
        chip_out[c] = (total[chunk_of(core, c), :] + pair_in[c].astype(f4)).astype(bf)
        to_chip(e).start()
    mine = total[chunk_of(core, chip), :] + pair_in[chip].astype(f4)
    for e in range(1, chips):
        from_chip(e).wait_recv()
        mine = mine + chip_in[behind[e]].astype(f4)
    done[core, chip] = mine.astype(bf)

    def spread(e):
        return remote(
            done.at[core, chip], done.at[core, chip], done_send.at[e], done_recv.at[chip],
            on_chip(near[e]),
        )

    def spread_from(e):
        c = behind[e]
        return remote(
            done.at[core, c], done.at[core, c], done_send.at[e], done_recv.at[c], on_chip(c)
        )

    def pass_on(c):
        return remote(done.at[core, c], done.at[core, c], mate_send.at[c], mate_recv.at[c], mate)

    def passed(c):
        return remote(
            done.at[1 - core, c], done.at[1 - core, c], mate_send.at[c], mate_recv.at[c], mate
        )

    for e in range(1, chips):
        spread(e).start()
    pass_on(chip).start()
    for e in range(1, chips):
        spread_from(e).wait_recv()
        pass_on(behind[e]).start()
    for e in range(chips):
        passed(behind[e]).wait_recv()
    for k in range(CORES):
        for c in range(chips):
            out_ref[k, c] = done[k, c]
    for e in range(chips):
        pass_on(behind[e]).wait_send()
    for e in range(1, chips):
        spread(e).wait_send()
        to_chip(e).wait_send()
    pair.wait_send()
    for d in range(1, tile_count):
        for buffers in (ask, pars, feats, grads, dpars):
            give(*buffers, d).wait_send()


def splat(
    block_list, block_home, pads, offset, centers, log_scales, correlation, opacity_logit,
    features, cotangent, tile_count, views, capacity,
):
    _, tiles, pixels, width = cotangent.shape
    shard_blocks, gauss, _ = features.shape
    length = block_list.shape[2]
    slots = tiles * length
    spaces = tile_count * capacity
    chunk = 256
    steps = tiles * (pixels // chunk)
    total = slots * gauss
    depth = gauss + ROWS
    chips = views // CORES
    part = -(-shard_blocks * depth // (views * 16)) * 16
    bf, f4, i4 = jnp.bfloat16, jnp.float32, jnp.int32
    dma = pltpu.SemaphoreType.DMA
    each = dma((tile_count,))
    args = (
        block_list, block_home, pads, offset, centers, log_scales, correlation, opacity_logit,
        features, cotangent,
    )
    held = [pltpu.SMEM(a.shape, a.dtype) for a in args[:4]]
    held += [pltpu.VMEM(a.shape, a.dtype) for a in args[4:]]
    held += [dma((len(args),))]
    held += [
        pltpu.SMEM((slots,), i4), pltpu.SMEM((slots,), i4), pltpu.SMEM((spaces,), i4),
        pltpu.VMEM((tile_count, 8, 128), i4), pltpu.VMEM((tile_count, 8, 128), i4),
        pltpu.VMEM((8, 128), i4), pltpu.SMEM((8, 128), i4), dma, each, each,
        pltpu.VMEM((shard_blocks, ROWS, gauss), f4),
    ]
    held += [pltpu.VMEM((tile_count, capacity, ROWS, gauss), bf)] * 2
    held += [pltpu.VMEM((tile_count, capacity, gauss, width), bf)] * 2
    held += [each] * 4
    held += [
        pltpu.VMEM((slots, gauss, width), bf),
        pltpu.VMEM((slots, ROWS, gauss), f4),
        pltpu.VMEM((tiles, width, length * gauss), bf),
        pltpu.VMEM((total, 32), bf),
        pltpu.VMEM((32, pixels), bf),
        pltpu.VMEM((pixels, 128), bf),
        pltpu.VMEM((PAIR * gauss, PAIR * gauss), bf),
        pltpu.VMEM((PAIR * gauss, PAIR * gauss), bf),
        pltpu.VMEM((steps, length * gauss, chunk), bf),
        pltpu.VMEM((steps, length * gauss, chunk), f4),
        pltpu.VMEM((steps, length * gauss, chunk), f4),
        pltpu.VMEM((total, 128), f4),
        pltpu.VMEM((slots, gauss, width), f4),
        pltpu.VMEM((slots, 8, gauss), f4),
    ]
    held += [pltpu.VMEM((tile_count, capacity, gauss, width), bf)] * 2
    held += [pltpu.VMEM((tile_count, capacity, 8, gauss), f4)] * 2
    held += [each] * 4
    held += [pltpu.VMEM((views * part, gauss), f4)]
    held += [pltpu.VMEM((chips, part, gauss), bf)] * 4
    held += [pltpu.VMEM((CORES, chips, part, gauss), bf)]
    held += [dma((2,))] + [dma((chips,))] * 6
    return pl.pallas_call(
        functools.partial(splat_kernel, capacity, chunk),
        out_shape=(
            jax.ShapeDtypeStruct(cotangent.shape, bf),
            jax.ShapeDtypeStruct((CORES, chips, part, gauss), bf),
        ),
        in_specs=[ANY] * len(args),
        out_specs=(VMEM, VMEM),
        scratch_shapes=held,
        compiler_params=pltpu.CompilerParams(
            collective_id=0, has_side_effects=True, vmem_limit_bytes=58 * 2**20
        ),
        name="splat",
    )(*args)


def unpack_kernel(all_ref, centers_ref, scales_ref, corr_ref, opac_ref, feat_ref):
    shard_blocks, width, _ = feat_ref.shape
    depth = width + ROWS
    for r in range(shard_blocks):
        feat_ref[r] = all_ref[r * depth:r * depth + width, :].astype(jnp.float32)
        par = all_ref[r * depth + width:(r + 1) * depth, :].astype(jnp.float32)
        centers_ref[r] = par[0:2]
        scales_ref[r] = par[2:4]
        corr_ref[r:r + 1, :] = par[4:5]
        opac_ref[r:r + 1, :] = par[5:6]


def unpack(everything, shard_blocks, width, gauss):
    f4 = jnp.float32
    return pl.pallas_call(
        unpack_kernel,
        out_shape=(
            jax.ShapeDtypeStruct((shard_blocks, 2, gauss), f4),
            jax.ShapeDtypeStruct((shard_blocks, 2, gauss), f4),
            jax.ShapeDtypeStruct((shard_blocks, gauss), f4),
            jax.ShapeDtypeStruct((shard_blocks, gauss), f4),
            jax.ShapeDtypeStruct((shard_blocks, width, gauss), f4),
        ),
        in_specs=[VMEM],
        out_specs=(VMEM,) * 5,
        compiler_params=pltpu.CompilerParams(vmem_limit_bytes=32 * 2**20),
        name="unpack",
    )(everything)


def shards(
    centers, log_scales, correlation, opacity_logit, features,
    view_offset, block_list, pad_count, block_home, image_grad,
):
    tile_count = lax.axis_size("tile")
    views = lax.axis_size("view")
    shard_blocks, gauss, width = features.shape
    slot_count = block_list.shape[1] * block_list.shape[2]
    capacity = (slot_count + tile_count - 1) // tile_count + 1
    image, summed = splat(
        block_list, block_home, pad_count, view_offset, centers, log_scales, correlation,
        opacity_logit, features, image_grad, tile_count, views, capacity,
    )
    return (image,) + tuple(unpack(summed.reshape(-1, gauss), shard_blocks, width, gauss))


def solution(mesh):
    in_specs = (
        P("tile", None, None),
        P("tile", None, None),
        P("tile", None),
        P("tile", None),
        P("tile", None, None),
        P("view", None),
        P("view", "tile", None),
        P("view", "tile"),
        P(),
        P("view", "tile", None, None),
    )
    out_specs = (
        P("view", "tile", None, None),
        P("tile", None, None),
        P("tile", None, None),
        P("tile", None),
        P("tile", None),
        P("tile", None, None),
    )
    return jax.shard_map(shards, mesh=mesh, in_specs=in_specs, out_specs=out_specs, check_vma=False)
```

time: 824 us -> 77.9 us (0.09); the launches traced: 808 us -> 77.7 us
  other arithmetic: 285 us -> 0 us
  local copies, waits for them, and re-layouts: 219 us -> 3.03 us
  waiting for transfers between devices: 124 us -> 0 us
  matrix products: 79.5 us -> 0 us
  Pallas kernels: 0 us -> 74 us
  blocking collectives: 54.9 us -> 0 us
  starting transfers between devices: 24.5 us -> 0 us
  between operations: 15.9 us -> 0.65 us
    another operation x67 -> x0, other arithmetic: 157 us -> none  [the longest x48 157 us: block_step(): before = jnp.cumsum(log_keep, axis=1) - log_keep]
    dynamic_update_slice x96 -> x0, local copies, waits for them, and re-layouts: 120 us -> none  [render_tile(): lax.scan(jax.checkpoint(block_step), start_state, tuple(tensors) + (alive...]
    psum x2 -> x0, waiting for transfers between devices: 90.3 us -> none  [shards(): lax.psum((shard_grads[0], shard_grads[1], shard_grads[2], shard_grads[3],...]
    dot_general x58 -> x0, matrix products: 79.5 us -> none  [the longest x48 68 us: block_step(): jnp.dot(weight, feature.astype(jnp.bfloat16), preferred_element_type=jnp....]
    pallas_call x0 -> x2, Pallas kernels: none -> 74 us  [the longest x1 72.7 us: splat(): pl.pallas_call(functools.partial(splat_kernel, capacity, chunk), out_shap...]
    all_gather x4 -> x0, blocking collectives: 54.9 us -> none  [the longest x1 14.1 us: shards(): lax.all_gather(correlation, 'tile', axis=0, tiled=True)]
    log1p x32 -> x0, other arithmetic: 36.6 us -> none  [block_step(): log_keep = jnp.log1p(-alphas)]
    dynamic_slice x64 -> x0, local copies, waits for them, and re-layouts: 33.6 us -> none  [render_tile(): lax.scan(jax.checkpoint(block_step), start_state, tuple(tensors) + (alive...]
  transfers between devices with their start and end apart: 9 -> 0, of which waited for: 7 -> 0; matrix products, arithmetic and copies ran while one was open for 71% -> 0% of each run, Pallas kernels for 0% -> 0%
where the time goes in v2:
time: 77.9 us; the launch traced here: 77.7 us
  Pallas kernels  74 us (95%)
  local copies, waits for them, and re-layouts  3.03 us (4%)
    pallas_call x1, Pallas kernels, splat(): pl.pallas_call(functools.partial(splat_kernel, capacity, chunk), out_shap...  72.7 us
    unnamed x3, local copies, waits for them, and re-layouts  3.03 us

profile of v2, /device:TPU:0, one launch (start us, length us, event | category | flops | bytes accessed | tf_op | source)
XLA Modules:
  0.0 77.7 jit_solution(14787788385557277354)
XLA Ops:
  0.6 72.7 %splat.1 = (bf16[1,2,1024,128]{3,2,1,0:T(8,128)(2,1)}, bf16[2,4,432,128]{3,2,1,0:T(8,128)(2,1)}) custom-call(s32[1,2,8]{2,1,0:T(2,128)} %list_hbm.1, s32[96]{0:T(128)} %home_hbm.1, s32[1,2]{1,0:T(1,128)} %pad_hbm.1, f32[1,2]{1,0:T(1,128)} %off_hbm.1, bf16[24,2,128]{2,1,0:T(2,128)(2,1)} %centers_hbm.1, bf16[24,2,128]{2,1,0:T(2,128)(2,1)} %scales_hbm.1, ...), custom_call_target="tpu_custom_call" | custom-call | tf_op jit(solution)/shard_map/splat/pallas_call | solution.py:505
  73.4 0.0 copy-start
  73.4 1.2 %copy-done = bf16[2,4,432,128]{3,2,1,0:T(8,128)(2,1)S(1)} copy-done((bf16[2,4,432,128]{3,2,1,0:T(8,128)(2,1)S(1)}, bf16[2,4,432,128]{3,2,1,0:T(8,128)(2,1)}, u32[]{:S(2)}) %copy-start) | copy-done | bytes 884760
  74.5 1.3 %unpack.1 = (f32[24,2,128]{2,1,0:T(2,128)}, f32[24,2,128]{2,1,0:T(2,128)}, f32[24,128]{1,0:T(8,128)}, f32[24,128]{1,0:T(8,128)}, f32[24,128,128]{2,1,0:T(8,128)}) custom-call(bf16[3456,128]{1,0:T(8,128)(2,1)S(1)} %bitcast.1), custom_call_target="tpu_custom_call" | custom-call | tf_op jit(solution)/shard_map/unpack/pallas_call | solution.py:535
  75.8 1.9 %copy.17 = bf16[1,2,1024,128]{3,2,1,0:T(8,128)(2,1)} copy(bf16[1,2,1024,128]{3,2,1,0:T(8,128)(2,1)} %get-tuple-element.26) | data formatting | bytes 1048576
Async XLA Ops:
  73.4 1.2 %copy-start = (bf16[2,4,432,128]{3,2,1,0:T(8,128)(2,1)S(1)}, bf16[2,4,432,128]{3,2,1,0:T(8,128)(2,1)}, u32[]{:S(2)}) copy-start(bf16[2,4,432,128]{3,2,1,0:T(8,128)(2,1)} %get-tuple-element.14) | copy-start | bytes 2654212

commit v3 on v2

--- a/solution.py
+++ b/solution.py
@@ -11,6 +11,7 @@
 ROWS = 16
 PAIR = 2
 CORES = 2
+PIECES = 4
 LOG2E = 1.4426950408889634
 SMEM = pl.BlockSpec(memory_space=pltpu.SMEM)
 VMEM = pl.BlockSpec(memory_space=pltpu.VMEM)
@@ -65,7 +66,7 @@
     capacity, chunk,
     list_hbm, home_hbm, pad_hbm, off_hbm, centers_hbm, scales_hbm, corr_hbm, opac_hbm,
     feat_hbm, cot_hbm,
-    image_ref, out_ref,
+    image_ref, out_ref, out_par_ref,
     list_ref, home_ref, pad_ref, off_ref, centers_ref, scales_ref, corr_ref, opac_ref,
     feat_ref, cot_ref, in_sem,
     at_ref, owner_ref, slot_ref, req, req_in, table_v, table, table_sem, req_send, req_recv,
@@ -75,6 +76,7 @@
     weight, exact, ratio, moment, dfeat, dpar,
     grad_out, grad_in, dpar_out, dpar_in, grad_send, grad_recv, dpar_send, dpar_recv,
     total, pair_out, pair_in, chip_out, chip_in, done,
+    total_p, pair_out_p, pair_in_p, chip_out_p, chip_in_p, done_p,
     pair_sem, chip_send, chip_recv, done_send, done_recv, mate_send, mate_recv,
 ):
     _, tiles, length = list_ref.shape
@@ -82,12 +84,12 @@
     slots = tiles * length
     shard_blocks, gauss, width = feat_ref.shape
     tile_count = req.shape[0]
-    depth = gauss + ROWS
     span = PAIR * gauss
     pairs = length // PAIR
     chunks = pixels // chunk
-    _, chips, part, _ = done.shape
-    half = chips * part
+    steps = tiles * chunks
+    chips = done.shape[2]
+    piece = gauss // PIECES
     bf, f4 = jnp.bfloat16, jnp.float32
 
     me = lax.axis_index("tile")
@@ -113,7 +115,10 @@
     ask = (req, req_in, req_send, req_recv)
     pars = (par_out, par_in, par_send, par_recv)
     feats = (feat_out, feat_in, feat_send, feat_recv)
-    grads = (grad_out, grad_in, grad_send, grad_recv)
+    grads = [
+        tuple(ref.at[k] for ref in (grad_out, grad_in, grad_send, grad_recv))
+        for k in range(PIECES)
+    ]
     dpars = (dpar_out, dpar_in, dpar_send, dpar_recv)
 
     loads = [
@@ -273,15 +278,18 @@
         slot = slot_ref[q]
         return jnp.where(slot > 0, grad_ref[jnp.maximum(slot - 1, 0)], 0.0)
 
-    for d in list(range(1, tile_count)) + [0]:
-        for c in range(capacity):
-            got = outgoing(dfeat, peers[d] * capacity + c).astype(bf)
+    for k in range(PIECES):
+        for d in list(range(1, tile_count)) + [0]:
+            for c in range(capacity):
+                slot = slot_ref[peers[d] * capacity + c]
+                got = dfeat[jnp.maximum(slot - 1, 0), k * piece:(k + 1) * piece, :]
+                got = jnp.where(slot > 0, got, 0.0).astype(bf)
+                if d:
+                    grad_out[k, peers[d], c] = got
+                else:
+                    grad_in[k, me, c] = got
             if d:
-                grad_out[peers[d], c] = got
-            else:
-                grad_in[me, c] = got
-        if d:
-            give(*grads, d).start()
+                give(*grads[k], d).start()
 
     for d in range(1, tile_count):
         given(*feats, d).wait_recv()
@@ -311,7 +319,144 @@
         image_ref[0, tile, pl.ds(start, chunk), :] = image.T.astype(bf)
         return carry
 
-    lax.fori_loop(0, tiles * chunks, backward, 0)
+    def add_features(k):
+        for d in range(1, tile_count):
+            given(*grads[k], d).wait_recv()
+        if total.shape[1] > shard_blocks * piece:
+            total[k] = jnp.zeros(total.shape[1:], f4)
+
+        def add(r, carry):
+            acc = jnp.zeros((piece, width), f4)
+            for t in range(tile_count):
+                for c in range(capacity):
+                    mark = jnp.where(table[0, t * capacity + c] == r + 1, 1.0, 0.0)
+                    acc = acc + mark * grad_in[k, t, c].astype(f4)
+            total[k, pl.ds(pl.multiple_of(r * piece, 16), piece), :] = acc
+            return carry
+
+        lax.fori_loop(0, shard_blocks, add, 0)
+
+    def add_params():
+        for d in range(1, tile_count):
+            given(*dpars, d).wait_recv()
+        total_p[...] = jnp.zeros_like(total_p)
+
+        def add(r, carry):
+            acc = jnp.zeros(dpar_in.shape[2:], f4)
+            for t in range(tile_count):
+                for c in range(capacity):
+                    mark = jnp.where(table[0, t * capacity + c] == r + 1, 1.0, 0.0)
+                    acc = acc + mark * dpar_in[t, c]
+            total_p[pl.ds(pl.multiple_of(r * 8, 8), 8), :] = acc
+            return carry
+
+        lax.fori_loop(0, shard_blocks, add, 0)
+
+    stage_count = 5
+
+    def buffers_of(k):
+        if k < PIECES:
+            held = (total, pair_out, pair_in, chip_out, chip_in, done, out_ref)
+            return tuple(ref.at[k] for ref in held)
+        return total_p, pair_out_p, pair_in_p, chip_out_p, chip_in_p, done_p, out_par_ref
+
+    def moves(k):
+        _, p_out, p_in, c_out, c_in, fin, _ = buffers_of(k)
+
+        def to_mate():
+            return remote(p_out, p_in, pair_sem.at[k, 0], pair_sem.at[k, 1], mate)
+
+        def to_chip(e):
+            return remote(
+                c_out.at[near[e]], c_in.at[chip], chip_send.at[k, e], chip_recv.at[k, chip],
+                on_chip(near[e]),
+            )
+
+        def from_chip(e):
+            c = behind[e]
+            return remote(
+                c_out.at[c], c_in.at[c], chip_send.at[k, e], chip_recv.at[k, c], on_chip(c)
+            )
+
+        def spread(e):
+            return remote(
+                fin.at[core, chip], fin.at[core, chip], done_send.at[k, e],
+                done_recv.at[k, chip], on_chip(near[e]),
+            )
+
+        def spread_from(e):
+            c = behind[e]
+            return remote(
+                fin.at[core, c], fin.at[core, c], done_send.at[k, e], done_recv.at[k, c],
+                on_chip(c),
+            )
+
+        def pass_on(c):
+            return remote(
+                fin.at[core, c], fin.at[core, c], mate_send.at[k, c], mate_recv.at[k, c], mate
+            )
+
+        def passed(c):
+            return remote(
+                fin.at[1 - core, c], fin.at[1 - core, c], mate_send.at[k, c],
+                mate_recv.at[k, c], mate,
+            )
+
+        return to_mate, to_chip, from_chip, spread, spread_from, pass_on, passed
+
+    def advance(k, stage):
+        tot, p_out, p_in, c_out, c_in, fin, out = buffers_of(k)
+        to_mate, to_chip, from_chip, spread, spread_from, pass_on, passed = moves(k)
+        part = fin.shape[2]
+
+        def chunk_of(which, c):
+            return pl.ds(pl.multiple_of((which * chips + c) * part, 16), part)
+
+        if stage == 0:
+            if k < PIECES:
+                add_features(k)
+            else:
+                add_params()
+            for c in range(chips):
+                p_out[c] = tot[chunk_of(1 - core, c), :].astype(bf)
+            to_mate().start()
+        elif stage == 1:
+            to_mate().wait_recv()
+            for e in range(1, chips):
+                c = near[e]
+                c_out[c] = (tot[chunk_of(core, c), :] + p_in[c].astype(f4)).astype(bf)
+                to_chip(e).start()
+        elif stage == 2:
+            mine = tot[chunk_of(core, chip), :] + p_in[chip].astype(f4)
+            for e in range(1, chips):
+                from_chip(e).wait_recv()
+                mine = mine + c_in[behind[e]].astype(f4)
+            fin[core, chip] = mine.astype(bf)
+            for e in range(1, chips):
+                spread(e).start()
+            pass_on(chip).start()
+        elif stage == 3:
+            for e in range(1, chips):
+                spread_from(e).wait_recv()
+                pass_on(behind[e]).start()
+        else:
+            for e in range(chips):
+                passed(behind[e]).wait_recv()
+            for which in range(CORES):
+                for c in range(chips):
+                    out[which, c] = fin[which, c]
+
+    def tick(t):
+        for k in range(PIECES + 1):
+            if 0 <= t - k < stage_count:
+                advance(k, t - k)
+
+    phases = PIECES if steps % PIECES == 0 else 1
+    for phase in range(phases):
+        each = steps // phases
+        lax.fori_loop(phase * each, (phase + 1) * each, backward, 0)
+        if 0 < phase:
+            tick(phase - 1)
 
     def finish(s, carry):
         x, y, a, b, c, root = gaussian_terms(prm[s], off_x, off_y)
@@ -341,107 +486,18 @@
         if d:
             give(*dpars, d).start()
 
-    total[...] = jnp.zeros_like(total)
-    for d in range(tile_count):
-        if d:
-            given(*grads, d).wait_recv()
-        source = sources[d]
-        marks = [table[0, source * capacity + c] for c in range(capacity)]
-
-        def add(r, carry):
-            at = pl.ds(pl.multiple_of(r * depth, 16), gauss)
-            acc = total[at, :]
-            for c in range(capacity):
-                mark = jnp.where(marks[c] == r + 1, 1.0, 0.0)
-                acc = acc + mark * grad_in[source, c].astype(f4)
-            total[at, :] = acc
-            return carry
-
-        lax.fori_loop(0, shard_blocks, add, 0)
+    for t in range(phases - 1, PIECES + stage_count):
+        tick(t)
+    for k in range(PIECES + 1):
+        to_mate, to_chip, _, spread, _, pass_on, _ = moves(k)
+        to_mate().wait_send()
+        for e in range(1, chips):
+            to_chip(e).wait_send()
+            spread(e).wait_send()
+        for e in range(chips):
+            pass_on(behind[e]).wait_send()
     for d in range(1, tile_count):
-        given(*dpars, d).wait_recv()
-
-    def add_par(r, carry):
-        acc = jnp.zeros(dpar_in.shape[2:], f4)
-        for t in range(tile_count):
-            for c in range(capacity):
-                mark = jnp.where(table[0, t * capacity + c] == r + 1, 1.0, 0.0)
-                acc = acc + mark * dpar_in[t, c]
-        total[pl.ds(pl.multiple_of(r * depth + gauss, 16), 8), :] = acc
-        return carry
-
-    lax.fori_loop(0, shard_blocks, add_par, 0)
-
-    def chunk_of(k, c):
-        return pl.ds(pl.multiple_of((k * chips + c) * part, 16), part)
-
-    for c in range(chips):
-        pair_out[c] = total[chunk_of(1 - core, c), :].astype(bf)
-    pair = remote(pair_out, pair_in, pair_sem.at[0], pair_sem.at[1], mate)
-    pair.start()
-    pair.wait_recv()
-
-    def to_chip(e):
-        return remote(
-            chip_out.at[near[e]], chip_in.at[chip], chip_send.at[e], chip_recv.at[chip],
-            on_chip(near[e]),
-        )
-
-    def from_chip(e):
-        return remote(
-            chip_out.at[behind[e]], chip_in.at[behind[e]], chip_send.at[e],
-            chip_recv.at[behind[e]], on_chip(behind[e]),
-        )
-
-    for e in range(1, chips):
-        c = near[e]
-        chip_out[c] = (total[chunk_of(core, c), :] + pair_in[c].astype(f4)).astype(bf)
-        to_chip(e).start()
-    mine = total[chunk_of(core, chip), :] + pair_in[chip].astype(f4)
-    for e in range(1, chips):
-        from_chip(e).wait_recv()
-        mine = mine + chip_in[behind[e]].astype(f4)
-    done[core, chip] = mine.astype(bf)
-
-    def spread(e):
-        return remote(
-            done.at[core, chip], done.at[core, chip], done_send.at[e], done_recv.at[chip],
-            on_chip(near[e]),
-        )
-
-    def spread_from(e):
-        c = behind[e]
-        return remote(
-            done.at[core, c], done.at[core, c], done_send.at[e], done_recv.at[c], on_chip(c)
-        )
-
-    def pass_on(c):
-        return remote(done.at[core, c], done.at[core, c], mate_send.at[c], mate_recv.at[c], mate)
-
-    def passed(c):
-        return remote(
-            done.at[1 - core, c], done.at[1 - core, c], mate_send.at[c], mate_recv.at[c], mate
-        )
-
-    for e in range(1, chips):
-        spread(e).start()
-    pass_on(chip).start()
-    for e in range(1, chips):
-        spread_from(e).wait_recv()
-        pass_on(behind[e]).start()
-    for e in range(chips):
-        passed(behind[e]).wait_recv()
-    for k in range(CORES):
-        for c in range(chips):
-            out_ref[k, c] = done[k, c]
-    for e in range(chips):
-        pass_on(behind[e]).wait_send()
-    for e in range(1, chips):
-        spread(e).wait_send()
-        to_chip(e).wait_send()
-    pair.wait_send()
-    for d in range(1, tile_count):
-        for buffers in (ask, pars, feats, grads, dpars):
+        for buffers in [ask, pars, feats, dpars] + grads:
             give(*buffers, d).wait_send()
 
 
@@ -457,9 +513,10 @@
     chunk = 256
     steps = tiles * (pixels // chunk)
     total = slots * gauss
-    depth = gauss + ROWS
+    piece = gauss // PIECES
     chips = views // CORES
-    part = -(-shard_blocks * depth // (views * 16)) * 16
+    part = -(-shard_blocks * piece // (views * 16)) * 16
+    part_p = -(-shard_blocks * 8 // (views * 16)) * 16
     bf, f4, i4 = jnp.bfloat16, jnp.float32, jnp.int32
     dma = pltpu.SemaphoreType.DMA
     each = dma((tile_count,))
@@ -495,21 +552,25 @@
         pltpu.VMEM((slots, gauss, width), f4),
         pltpu.VMEM((slots, 8, gauss), f4),
     ]
-    held += [pltpu.VMEM((tile_count, capacity, gauss, width), bf)] * 2
+    held += [pltpu.VMEM((PIECES, tile_count, capacity, piece, width), bf)] * 2
     held += [pltpu.VMEM((tile_count, capacity, 8, gauss), f4)] * 2
-    held += [each] * 4
-    held += [pltpu.VMEM((views * part, gauss), f4)]
-    held += [pltpu.VMEM((chips, part, gauss), bf)] * 4
-    held += [pltpu.VMEM((CORES, chips, part, gauss), bf)]
-    held += [dma((2,))] + [dma((chips,))] * 6
+    held += [dma((PIECES, tile_count))] * 2 + [each] * 2
+    held += [pltpu.VMEM((PIECES, views * part, width), f4)]
+    held += [pltpu.VMEM((PIECES, chips, part, width), bf)] * 4
+    held += [pltpu.VMEM((PIECES, CORES, chips, part, width), bf)]
+    held += [pltpu.VMEM((views * part_p, gauss), f4)]
+    held += [pltpu.VMEM((chips, part_p, gauss), bf)] * 4
+    held += [pltpu.VMEM((CORES, chips, part_p, gauss), bf)]
+    held += [dma((PIECES + 1, 2))] + [dma((PIECES + 1, chips))] * 6
     return pl.pallas_call(
         functools.partial(splat_kernel, capacity, chunk),
         out_shape=(
             jax.ShapeDtypeStruct(cotangent.shape, bf),
-            jax.ShapeDtypeStruct((CORES, chips, part, gauss), bf),
+            jax.ShapeDtypeStruct((PIECES, CORES, chips, part, width), bf),
+            jax.ShapeDtypeStruct((CORES, chips, part_p, gauss), bf),
         ),
         in_specs=[ANY] * len(args),
-        out_specs=(VMEM, VMEM),
+        out_specs=(VMEM, VMEM, VMEM),
         scratch_shapes=held,
         compiler_params=pltpu.CompilerParams(
             collective_id=0, has_side_effects=True, vmem_limit_bytes=58 * 2**20
@@ -518,34 +579,58 @@
     )(*args)
 
 
-def unpack_kernel(all_ref, centers_ref, scales_ref, corr_ref, opac_ref, feat_ref):
-    shard_blocks, width, _ = feat_ref.shape
-    depth = width + ROWS
+def unpack_kernel(
+    image_hbm, sums_hbm, par_hbm,
+    image_ref, centers_ref, scales_ref, corr_ref, opac_ref, feat_ref, sums, par, sem,
+):
+    shard_blocks, gauss, _ = feat_ref.shape
+    pieces = sums.shape[0]
+    piece = gauss // pieces
+    move = local(image_hbm, image_ref, sem.at[0])
+    move.start()
+    loads = [local(par_hbm, par, sem.at[1])]
+    loads += [local(sums_hbm.at[k], sums.at[k], sem.at[2 + k]) for k in range(pieces)]
+    for load in loads:
+        load.start()
+    loads[0].wait()
+    wide = par[...].astype(jnp.float32)
     for r in range(shard_blocks):
-        feat_ref[r] = all_ref[r * depth:r * depth + width, :].astype(jnp.float32)
-        par = all_ref[r * depth + width:(r + 1) * depth, :].astype(jnp.float32)
-        centers_ref[r] = par[0:2]
-        scales_ref[r] = par[2:4]
-        corr_ref[r:r + 1, :] = par[4:5]
-        opac_ref[r:r + 1, :] = par[5:6]
-
-
-def unpack(everything, shard_blocks, width, gauss):
+        row = wide[r * 8:(r + 1) * 8]
+        centers_ref[r] = row[0:2]
+        scales_ref[r] = row[2:4]
+        corr_ref[r:r + 1, :] = row[4:5]
+        opac_ref[r:r + 1, :] = row[5:6]
+    for k in range(pieces):
+        loads[1 + k].wait()
+        for r in range(shard_blocks):
+            feat_ref[r, k * piece:(k + 1) * piece, :] = (
+                sums[k, r * piece:(r + 1) * piece, :].astype(jnp.float32)
+            )
+    move.wait()
+
+
+def unpack(image, sums, par, shard_blocks, width, gauss):
     f4 = jnp.float32
     return pl.pallas_call(
         unpack_kernel,
         out_shape=(
+            jax.ShapeDtypeStruct(image.shape, image.dtype),
             jax.ShapeDtypeStruct((shard_blocks, 2, gauss), f4),
             jax.ShapeDtypeStruct((shard_blocks, 2, gauss), f4),
             jax.ShapeDtypeStruct((shard_blocks, gauss), f4),
             jax.ShapeDtypeStruct((shard_blocks, gauss), f4),
-            jax.ShapeDtypeStruct((shard_blocks, width, gauss), f4),
+            jax.ShapeDtypeStruct((shard_blocks, gauss, width), f4),
         ),
-        in_specs=[VMEM],
-        out_specs=(VMEM,) * 5,
-        compiler_params=pltpu.CompilerParams(vmem_limit_bytes=32 * 2**20),
+        in_specs=[ANY] * 3,
+        out_specs=(ANY,) + (VMEM,) * 5,
+        scratch_shapes=[
+            pltpu.VMEM(sums.shape, sums.dtype),
+            pltpu.VMEM(par.shape, par.dtype),
+            pltpu.SemaphoreType.DMA((2 + sums.shape[0],)),
+        ],
+        compiler_params=pltpu.CompilerParams(vmem_limit_bytes=58 * 2**20),
         name="unpack",
-    )(everything)
+    )(image, sums, par)
 
 
 def shards(
@@ -557,11 +642,12 @@
     shard_blocks, gauss, width = features.shape
     slot_count = block_list.shape[1] * block_list.shape[2]
     capacity = (slot_count + tile_count - 1) // tile_count + 1
-    image, summed = splat(
+    image, sums, par = splat(
         block_list, block_home, pad_count, view_offset, centers, log_scales, correlation,
         opacity_logit, features, image_grad, tile_count, views, capacity,
     )
-    return (image,) + tuple(unpack(summed.reshape(-1, gauss), shard_blocks, width, gauss))
+    sums = sums.reshape(sums.shape[0], -1, width)
+    return tuple(unpack(image, sums, par.reshape(-1, gauss), shard_blocks, width, gauss))
 
 
 def solution(mesh):

time: 77.9 us -> 95.4 us (1.22)
  Pallas kernels: 74 us -> 94.6 us
  local copies, waits for them, and re-layouts: 3.03 us -> 0 us
    pallas_call x1, Pallas kernels: 1.27 us -> 18.2 us  [unpack(): pl.pallas_call(unpack_kernel, out_shape=(jax.ShapeDtypeStruct(image.shape...]
    pallas_call x1, Pallas kernels: 72.7 us -> 76.4 us  [splat(): pl.pallas_call(functools.partial(splat_kernel, capacity, chunk), out_shap...]
    unnamed x3 -> x0, local copies, waits for them, and re-layouts: 3.03 us -> none
where the time goes in v3:
time: 95.4 us; the launch traced here: 95.2 us
  Pallas kernels  94.6 us (99%)
    pallas_call x1, Pallas kernels, splat(): pl.pallas_call(functools.partial(splat_kernel, capacity, chunk), out_shap...  76.4 us
    pallas_call x1, Pallas kernels, unpack(): pl.pallas_call(unpack_kernel, out_shape=(jax.ShapeDtypeStruct(image.shape...  18.2 us

profile of v3, /device:TPU:0, one launch (start us, length us, event | category | flops | bytes accessed | tf_op | source)
XLA Modules:
  0.0 95.2 jit_solution(17032117917487297495)
XLA Ops:
  0.6 76.4 %splat.1 = (bf16[1,2,1024,128]{3,2,1,0:T(8,128)(2,1)}, bf16[4,2,4,96,128]{4,3,2,1,0:T(8,128)(2,1)}, bf16[2,4,32,128]{3,2,1,0:T(8,128)(2,1)}) custom-call(s32[1,2,8]{2,1,0:T(2,128)} %list_hbm.1, s32[96]{0:T(128)} %home_hbm.1, s32[1,2]{1,0:T(1,128)} %pad_hbm.1, f32[1,2]{1,0:T(1,128)} %off_hbm.1, bf16[24,2,128]{2,1,0:T(2,128)(2,1)} %centers_hbm.1, ...), custom_call_target="tpu_custom_call" | custom-call | tf_op jit(solution)/shard_map/splat/pallas_call | solution.py:565
  77.0 18.2 %unpack.1 = (bf16[1,2,1024,128]{3,2,1,0:T(8,128)(2,1)}, f32[24,2,128]{2,1,0:T(2,128)}, f32[24,2,128]{2,1,0:T(2,128)}, f32[24,128]{1,0:T(8,128)}, f32[24,128]{1,0:T(8,128)}, /*index=5*/f32[24,128,128]{2,1,0:T(8,128)}) custom-call(bf16[1,2,1024,128]{3,2,1,0:T(8,128)(2,1)} %get-tuple-element.9.image_hbm, bf16[4,768,128]{2,1,0:T(8,128)(2,1)} %bitcast.2, ...), custom_call_target="tpu_custom_call" | custom-call | tf_op jit(solution)/shard_map/unpack/pallas_call | solution.py:614

commit v4 on v3

--- a/solution.py
+++ b/solution.py
@@ -11,7 +11,7 @@
 ROWS = 16
 PAIR = 2
 CORES = 2
-PIECES = 4
+PIECES = 2
 LOG2E = 1.4426950408889634
 SMEM = pl.BlockSpec(memory_space=pltpu.SMEM)
 VMEM = pl.BlockSpec(memory_space=pltpu.VMEM)
@@ -328,9 +328,11 @@
         def add(r, carry):
             acc = jnp.zeros((piece, width), f4)
             for t in range(tile_count):
+                some = jnp.zeros((piece, width), bf)
                 for c in range(capacity):
                     mark = jnp.where(table[0, t * capacity + c] == r + 1, 1.0, 0.0)
-                    acc = acc + mark * grad_in[k, t, c].astype(f4)
+                    some = some + mark.astype(bf) * grad_in[k, t, c]
+                acc = acc + some.astype(f4)
             total[k, pl.ds(pl.multiple_of(r * piece, 16), piece), :] = acc
             return carry
 
@@ -451,12 +453,7 @@
             if 0 <= t - k < stage_count:
                 advance(k, t - k)
 
-    phases = PIECES if steps % PIECES == 0 else 1
-    for phase in range(phases):
-        each = steps // phases
-        lax.fori_loop(phase * each, (phase + 1) * each, backward, 0)
-        if 0 < phase:
-            tick(phase - 1)
+    lax.fori_loop(0, steps, backward, 0)
 
     def finish(s, carry):
         x, y, a, b, c, root = gaussian_terms(prm[s], off_x, off_y)
@@ -486,7 +483,7 @@
         if d:
             give(*dpars, d).start()
 
-    for t in range(phases - 1, PIECES + stage_count):
+    for t in range(PIECES + stage_count):
         tick(t)
     for k in range(PIECES + 1):
         to_mate, to_chip, _, spread, _, pass_on, _ = moves(k)
@@ -581,17 +578,20 @@
 
 def unpack_kernel(
     image_hbm, sums_hbm, par_hbm,
-    image_ref, centers_ref, scales_ref, corr_ref, opac_ref, feat_ref, sums, par, sem,
+    image_ref, centers_ref, scales_ref, corr_ref, opac_ref, feat_ref, held, sums, par, sem,
 ):
     shard_blocks, gauss, _ = feat_ref.shape
     pieces = sums.shape[0]
     piece = gauss // pieces
-    move = local(image_hbm, image_ref, sem.at[0])
-    move.start()
+    bring = local(image_hbm, held, sem.at[0])
+    bring.start()
     loads = [local(par_hbm, par, sem.at[1])]
     loads += [local(sums_hbm.at[k], sums.at[k], sem.at[2 + k]) for k in range(pieces)]
     for load in loads:
         load.start()
+    bring.wait()
+    move = local(held, image_ref, sem.at[0])
+    move.start()
     loads[0].wait()
     wide = par[...].astype(jnp.float32)
     for r in range(shard_blocks):
@@ -624,6 +624,7 @@
         in_specs=[ANY] * 3,
         out_specs=(ANY,) + (VMEM,) * 5,
         scratch_shapes=[
+            pltpu.VMEM(image.shape, image.dtype),
             pltpu.VMEM(sums.shape, sums.dtype),
             pltpu.VMEM(par.shape, par.dtype),
             pltpu.SemaphoreType.DMA((2 + sums.shape[0],)),

time: 95.4 us -> 79.2 us (0.83)
  Pallas kernels: 94.6 us -> 78.4 us
    pallas_call x1, Pallas kernels: 18.2 us -> 3.04 us  [unpack(): pl.pallas_call(unpack_kernel, out_shape=(jax.ShapeDtypeStruct(image.shape...]
    pallas_call x1, Pallas kernels: 76.4 us -> 75.3 us  [splat(): pl.pallas_call(functools.partial(splat_kernel, capacity, chunk), out_shap...]
where the time goes in v4:
time: 79.2 us; the launch traced here: 79 us
  Pallas kernels  78.4 us (99%)
    pallas_call x1, Pallas kernels, splat(): pl.pallas_call(functools.partial(splat_kernel, capacity, chunk), out_shap...  75.3 us
    pallas_call x1, Pallas kernels, unpack(): pl.pallas_call(unpack_kernel, out_shape=(jax.ShapeDtypeStruct(image.shape...  3.04 us

profile of v4, /device:TPU:0, one launch (start us, length us, event | category | flops | bytes accessed | tf_op | source)
XLA Modules:
  0.0 79.0 jit_solution(2123316007573858335)
XLA Ops:
  0.6 75.3 %splat.1 = (bf16[1,2,1024,128]{3,2,1,0:T(8,128)(2,1)}, bf16[2,2,4,192,128]{4,3,2,1,0:T(8,128)(2,1)}, bf16[2,4,32,128]{3,2,1,0:T(8,128)(2,1)}) custom-call(s32[1,2,8]{2,1,0:T(2,128)} %list_hbm.1, s32[96]{0:T(128)} %home_hbm.1, s32[1,2]{1,0:T(1,128)} %pad_hbm.1, f32[1,2]{1,0:T(1,128)} %off_hbm.1, bf16[24,2,128]{2,1,0:T(2,128)(2,1)} %centers_hbm.1, ...), custom_call_target="tpu_custom_call" | custom-call | tf_op jit(solution)/shard_map/splat/pallas_call | solution.py:562
  76.0 3.0 %unpack.1 = (bf16[1,2,1024,128]{3,2,1,0:T(8,128)(2,1)}, f32[24,2,128]{2,1,0:T(2,128)}, f32[24,2,128]{2,1,0:T(2,128)}, f32[24,128]{1,0:T(8,128)}, f32[24,128]{1,0:T(8,128)}, /*index=5*/f32[24,128,128]{2,1,0:T(8,128)}) custom-call(bf16[1,2,1024,128]{3,2,1,0:T(8,128)(2,1)} %get-tuple-element.9.image_hbm, bf16[2,1536,128]{2,1,0:T(8,128)(2,1)} %bitcast.2, ...), custom_call_target="tpu_custom_call" | custom-call | tf_op jit(solution)/shard_map/unpack/pallas_call | solution.py:614
